TPU v7x, 512 devices: a whole 4x8x8 slice. The times are simulated.
512 devices in a mesh: grp: 16 (over z, core), row: 32 (over y, x).
Axes of the slice: x: 4, y: 8, z: 8, core: 2. Of those that a mesh axis runs over, the one named last changes fastest.
Arguments:
- leaf_rhs: float32 [32, 16, 256, 128], P('row', 'grp'), may hold values from -6 to 6
- leaf_inv: float32 [32, 16, 256, 256], P('row', 'grp'), may hold values from -0.15625 to 1.15625, as said below
- leaf_panel: float32 [32, 16, 6, 256, 256], P('row', 'grp'), may hold values from -0.15625 to 0.15625
- leaf_mask: int32 [32, 16, 6], P('row', 'grp'), may hold values 0 or 1
- inner_rhs: float32 [32, 256, 128], P('row', 'grp'), may hold values from -6 to 6
- inner_inv: float32 [32, 256, 256], P('row', 'grp'), may hold values from -0.15625 to 1.15625, as said below
- inner_panel: float32 [32, 6, 256, 256], P('row', None, 'grp'), may hold values from -0.15625 to 0.15625, as said below
Outputs:
- leaf_solution: float32 [32, 16, 256, 128], P('row', 'grp')
- inner_solution: float32 [32, 256, 128], P('row', 'grp')
Inputs may be any that keep to these rules, and one draw needn't show every extreme that they name: `leaf_inv`: identity plus a full matrix of independent entries; diagonal entries near 1, off-diagonal entries small. `inner_inv`: identity plus a full matrix of independent entries; diagonal entries near 1, off-diagonal entries small. `inner_panel`: blocks for levels at or below the supernode's own level are not used.
All inputs are finite; a program needn't handle non-finite values. No bound on the sum of `leaf_mask` on one device may be relied on, other than what follows from the above.
Results may differ from a plain program's by a relative error of at most 0.0003.
Values sent between devices are 32-bit elements; how exact they have to be, the bound alone decides.
A program may use at most 64 MiB of HBM per device.

v0:
```python
import jax
import jax.numpy as jnp
from jax import lax
from jax.sharding import PartitionSpec as P


def pick_slot(total, picks):
    return jnp.einsum("g,gnr->nr", picks, total, precision=lax.Precision.HIGHEST)


def per_device(leaf_rhs, leaf_inv, leaf_panel, leaf_mask, inner_rhs, inner_inv, inner_panel):
    highest = lax.Precision.HIGHEST
    count = lax.axis_size("row")
    levels = count.bit_length()
    depth = levels - 1
    device = lax.axis_index("row")
    member = lax.axis_index("grp")
    share = inner_rhs.shape[1]
    trailing = jnp.zeros((), jnp.int32)
    for bit_pos in range(1, depth + 1):
        trailing = trailing + (device % 2**bit_pos == 0).astype(jnp.int32)
    own_level = jnp.where(device == 0, levels, trailing + 1)
    inverse_full = lax.all_gather(inner_inv[0], "grp", axis=0, tiled=True)
    masked = leaf_panel[0] * leaf_mask[0].astype(jnp.float32)[:, :, None, None]
    leaf_fwd = jnp.einsum("lnk,lkr->lnr", leaf_inv[0], leaf_rhs[0], precision=highest)
    inner_fwd = jnp.zeros(inner_rhs.shape[1:], jnp.float32)
    for step in range(levels):
        level = step + 1
        span = min(2**level, count)
        groups = count // span
        below = (own_level < level).astype(jnp.float32)
        panel_now = inner_panel[0, step]
        masked_now = masked[:, step]
        current = inner_fwd

        def upward(
            start,
            rows,
            panel_now=panel_now,
            masked_now=masked_now,
            current=current,
            below=below,
            step=step,
        ):
            inner_term = lax.dot_general(
                panel_now, current, (((0,), (0,)), ((), ())), precision=highest
            )
            leaf_term = jnp.einsum("lna,lnr->ar", masked_now, leaf_fwd, precision=highest)
            return leaf_term + below * inner_term

        update = lax.psum_scatter(
            upward(jnp.int32(0), share * lax.axis_size("grp")),
            "grp",
            scatter_dimension=0,
            tiled=True,
        )
        picks = (jnp.arange(groups) == device // span).astype(jnp.float32)
        placed = picks[:, None, None] * update[None]
        update = pick_slot(lax.psum(placed, "row"), picks)
        pending = lax.all_gather(inner_rhs[0] - update, "grp", axis=0, tiled=True)
        solved = jnp.dot(inner_inv[0], pending, precision=highest)
        inner_fwd = jnp.where(own_level == level, solved, inner_fwd)
    inner_back = jnp.zeros(inner_rhs.shape[1:], jnp.float32)
    inner_acc = jnp.zeros(inner_rhs.shape[1:], jnp.float32)
    leaf_acc = jnp.zeros(leaf_fwd.shape, jnp.float32)
    own_cols = lax.dynamic_slice_in_dim(inverse_full, member * share, share, 1)
    for step in reversed(range(levels)):
        level = step + 1
        span = min(2**level, count)
        groups = count // span
        below = (own_level < level).astype(jnp.float32)
        owner = own_level == level
        rest = lax.all_gather(inner_fwd - inner_acc, "grp", axis=0, tiled=True)
        solved = lax.dot_general(own_cols, rest, (((0,), (0,)), ((), ())), precision=highest)
        inner_back = jnp.where(owner, solved, inner_back)
        owned = jnp.where(owner, solved, 0.0)
        picks = (jnp.arange(groups) == device // span).astype(jnp.float32)
        placed = picks[:, None, None] * owned[None]
        ancestor = pick_slot(lax.psum(placed, "row"), picks)
        ancestor_full = lax.all_gather(ancestor, "grp", axis=0, tiled=True)
        leaf_acc = leaf_acc + jnp.einsum(
            "lna,ar->lnr", masked[:, step], ancestor_full, precision=highest
        )
        inner_acc = inner_acc + below * jnp.dot(
            inner_panel[0, step], ancestor_full, precision=highest
        )
    leaf_back = jnp.einsum("lkn,lkr->lnr", leaf_inv[0], leaf_fwd - leaf_acc, precision=highest)
    return (leaf_back[None], inner_back[None])


def solution(mesh):
    in_specs = (
        P("row", "grp", None, None),
        P("row", "grp", None, None),
        P("row", "grp", None, None, None),
        P("row", "grp", None),
        P("row", "grp", None),
        P("row", "grp", None),
        P("row", None, "grp", None),
    )
    out_specs = (P("row", "grp", None, None), P("row", "grp", None))
    return jax.shard_map(
        per_device, mesh=mesh, in_specs=in_specs, out_specs=out_specs, check_vma=False
    )
```

profile of v0, /device:TPU:1, one launch (start us, length us, event | category | flops | bytes accessed | tf_op | source)
XLA Modules:
  0.0 2121.6 jit_solution(2478848698043543026)
XLA Ops:
  8.0 1.1 fusion.6
  9.1 1.3 fusion.19
  10.4 1.7 bitcast_multiply_fusion
  12.1 1.3 convolution_add_fusion.5
  13.4 62.1 %reduce-scatter.7.cloned.1.call-done = f32[16,128]{1,0:T(8,128)} async-done(((f32[256,128]{1,0:T(8,128)}), f32[16,128]{1,0:T(8,128)}) %reduce-scatter.7.cloned.1.call-update) | async-done | bytes 8208 | tf_op jit(solution)/shard_map/reduce_scatter | solution.py:51
  75.5 1.4 broadcast_multiply_fusion.1
  77.0 151.8 %all-reduce.5.cloned.1.call-done = f32[16,16,128]{2,1,0:T(8,128)} async-done(((f32[16,16,128]{2,1,0:T(8,128)}), f32[16,16,128]{2,1,0:T(8,128)}) %all-reduce.5.cloned.1.call-update) | async-done | bytes 131088 | tf_op jit(solution)/shard_map/psum | solution.py:59
  229.9 22.7 %all_gather.58 = f32[256,128]{1,0:T(8,128)S(1)} all-gather(f32[16,128]{1,0:T(8,128)S(1)} %bitcast_subtract_fusion.5), channel_id=1, replica_groups=mesh['grp'=16,'row'=32] {'grp'}, dimensions={0}, use_global_device_ids=true | all-gather | bytes 139264 | tf_op jit(solution)/shard_map/all_gather | solution.py:60
  253.2 1.3 convolution_add_fusion.6
  254.5 51.5 %reduce-scatter.9.cloned.1.call-done = f32[16,128]{1,0:T(8,128)} async-done(((f32[256,128]{1,0:T(8,128)}), f32[16,128]{1,0:T(8,128)}) %reduce-scatter.9.cloned.1.call-update) | async-done | bytes 8208 | tf_op jit(solution)/shard_map/reduce_scatter | solution.py:51
  306.0 1.4 broadcast_multiply_fusion.3
  307.5 149.8 %all-reduce.7.cloned.1.call-done = f32[8,16,128]{2,1,0:T(8,128)} async-done(((f32[8,16,128]{2,1,0:T(8,128)}), f32[8,16,128]{2,1,0:T(8,128)}) %all-reduce.7.cloned.1.call-update) | async-done | bytes 65552 | tf_op jit(solution)/shard_map/psum | solution.py:59
  458.3 22.9 %all_gather.59 = f32[256,128]{1,0:T(8,128)S(1)} all-gather(f32[16,128]{1,0:T(8,128)S(1)} %bitcast_subtract_fusion.4), channel_id=1, replica_groups=mesh['grp'=16,'row'=32] {'grp'}, dimensions={0}, use_global_device_ids=true | all-gather | bytes 139264 | tf_op jit(solution)/shard_map/all_gather | solution.py:60
  481.8 1.3 convolution_add_fusion.7
  483.2 51.5 %reduce-scatter.11.cloned.1.call-done = f32[16,128]{1,0:T(8,128)} async-done(((f32[256,128]{1,0:T(8,128)}), f32[16,128]{1,0:T(8,128)}) %reduce-scatter.11.cloned.1.call-update) | async-done | bytes 8208 | tf_op jit(solution)/shard_map/reduce_scatter | solution.py:51
  535.4 114.9 %psum.86 = f32[4,16,128]{2,1,0:T(8,128)S(1)} all-reduce(f32[4,16,128]{2,1,0:T(8,128)S(1)} %broadcast_multiply_fusion.5), channel_id=1, replica_groups=mesh['grp'=16,'row'=32] {'row'}, use_global_device_ids=true, to_apply=%region_5.6 | all-reduce | flops 8192 | bytes 65536 | tf_op jit(solution)/shard_map/psum | solution.py:59
  650.5 45.5 %all_gather.60 = f32[256,128]{1,0:T(8,128)S(1)} all-gather(f32[16,128]{1,0:T(8,128)S(1)} %bitcast_subtract_fusion.3), channel_id=1, replica_groups=mesh['grp'=16,'row'=32] {'grp'}, dimensions={0}, use_global_device_ids=true | all-gather | bytes 139264 | tf_op jit(solution)/shard_map/all_gather | solution.py:60
  696.6 1.3 convolution_add_fusion.8
  698.0 49.7 %reduce-scatter.13.cloned.1.call-done = f32[16,128]{1,0:T(8,128)} async-done(((f32[256,128]{1,0:T(8,128)}), f32[16,128]{1,0:T(8,128)}) %reduce-scatter.13.cloned.1.call-update) | async-done | bytes 8208 | tf_op jit(solution)/shard_map/reduce_scatter | solution.py:51
  748.4 114.9 %psum.87 = f32[2,16,128]{2,1,0:T(8,128)S(1)} all-reduce(f32[2,16,128]{2,1,0:T(8,128)S(1)} %broadcast_multiply_fusion.7), channel_id=1, replica_groups=mesh['grp'=16,'row'=32] {'row'}, use_global_device_ids=true, to_apply=%region_7.8 | all-reduce | flops 4096 | bytes 32768 | tf_op jit(solution)/shard_map/psum | solution.py:59
  863.5 45.5 %all_gather.61 = f32[256,128]{1,0:T(8,128)S(1)} all-gather(f32[16,128]{1,0:T(8,128)S(1)} %bitcast_subtract_fusion.2), channel_id=1, replica_groups=mesh['grp'=16,'row'=32] {'grp'}, dimensions={0}, use_global_device_ids=true | all-gather | bytes 139264 | tf_op jit(solution)/shard_map/all_gather | solution.py:60
  909.6 1.3 convolution_add_fusion.9
  910.9 49.7 %reduce-scatter.15.cloned.1.call-done = f32[16,128]{1,0:T(8,128)} async-done(((f32[256,128]{1,0:T(8,128)}), f32[16,128]{1,0:T(8,128)}) %reduce-scatter.15.cloned.1.call-update) | async-done | bytes 8208 | tf_op jit(solution)/shard_map/reduce_scatter | solution.py:51
  961.3 61.5 %psum.88 = f32[1,16,128]{2,1,0:T(8,128)S(1)} all-reduce(f32[1,16,128]{2,1,0:T(8,128)S(1)} %multiply_bitcast_fusion.3), channel_id=1, replica_groups=mesh['grp'=16,'row'=32] {'row'}, use_global_device_ids=true, to_apply=%region_9.10 | all-reduce | flops 2048 | bytes 16384 | tf_op jit(solution)/shard_map/psum | solution.py:59
  1022.8 31.9 %all_gather.62 = f32[256,128]{1,0:T(8,128)S(1)} all-gather(f32[16,128]{1,0:T(8,128)S(1)} %bitcast_subtract_fusion.1), channel_id=1, replica_groups=mesh['grp'=16,'row'=32] {'grp'}, dimensions={0}, use_global_device_ids=true | all-gather | bytes 139264 | tf_op jit(solution)/shard_map/all_gather | solution.py:60
  1055.3 1.3 convolution_add_fusion.10
  1056.7 16.9 all-gather
  1073.5 32.8 %reduce-scatter.17.cloned.1.call-done = f32[16,128]{1,0:T(8,128)} async-done(((f32[256,128]{1,0:T(8,128)}), f32[16,128]{1,0:T(8,128)}) %reduce-scatter.17.cloned.1.call-update) | async-done | bytes 8208 | tf_op jit(solution)/shard_map/reduce_scatter | solution.py:51
  1107.1 61.4 %psum.89 = f32[1,16,128]{2,1,0:T(8,128)S(1)} all-reduce(f32[1,16,128]{2,1,0:T(8,128)S(1)} %multiply_bitcast_fusion.2), channel_id=1, replica_groups=mesh['grp'=16,'row'=32] {'row'}, use_global_device_ids=true, to_apply=%region_11.12 | all-reduce | flops 2048 | bytes 16384 | tf_op jit(solution)/shard_map/psum | solution.py:59
  1168.5 31.9 %all_gather.63 = f32[256,128]{1,0:T(8,128)S(1)} all-gather(f32[16,128]{1,0:T(8,128)S(1)} %bitcast_subtract_fusion), channel_id=1, replica_groups=mesh['grp'=16,'row'=32] {'grp'}, dimensions={0}, use_global_device_ids=true | all-gather | bytes 139264 | tf_op jit(solution)/shard_map/all_gather | solution.py:60
  1200.6 16.4 all_gather.64
  1217.5 56.7 %psum.90 = f32[1,16,128]{2,1,0:T(8,128)S(1)} all-reduce(f32[1,16,128]{2,1,0:T(8,128)S(1)} %multiply_bitcast_fusion.1), channel_id=1, replica_groups=mesh['grp'=16,'row'=32] {'row'}, use_global_device_ids=true, to_apply=%region_12.13 | all-reduce | flops 2048 | bytes 16384 | tf_op jit(solution)/shard_map/psum | solution.py:79
  1274.3 28.4 %all-gather.1 = f32[1,256,128]{2,1,0:T(8,128)S(1)} all-gather(f32[1,16,128]{2,1,0:T(8,128)S(1)} %broadcast_multiply_fusion.9), channel_id=3, replica_groups=mesh['grp'=16,'row'=32] {'grp'}, dimensions={1}, use_global_device_ids=true | all-gather | bytes 139264 | tf_op jit(solution)/shard_map/all_gather | solution.py:80
  1303.3 16.5 all_gather.66
  1320.2 58.7 %psum.91 = f32[1,16,128]{2,1,0:T(8,128)S(1)} all-reduce(f32[1,16,128]{2,1,0:T(8,128)S(1)} %multiply_bitcast_fusion), channel_id=1, replica_groups=mesh['grp'=16,'row'=32] {'row'}, use_global_device_ids=true, to_apply=%region_13.14 | all-reduce | flops 2048 | bytes 16384 | tf_op jit(solution)/shard_map/psum | solution.py:79
  1378.9 28.7 %all-gather.2 = f32[1,256,128]{2,1,0:T(8,128)S(1)} all-gather(f32[1,16,128]{2,1,0:T(8,128)S(1)} %broadcast_multiply_fusion.8), channel_id=4, replica_groups=mesh['grp'=16,'row'=32] {'grp'}, dimensions={1}, use_global_device_ids=true | all-gather | bytes 139264 | tf_op jit(solution)/shard_map/all_gather | solution.py:80
  1408.2 16.4 all_gather.68
  1425.2 110.3 %psum.92 = f32[2,16,128]{2,1,0:T(8,128)S(1)} all-reduce(f32[2,16,128]{2,1,0:T(8,128)S(1)} %broadcast_multiply_fusion.6), channel_id=1, replica_groups=mesh['grp'=16,'row'=32] {'row'}, use_global_device_ids=true, to_apply=%region_14.15 | all-reduce | flops 4096 | bytes 32768 | tf_op jit(solution)/shard_map/psum | solution.py:79
  1535.7 41.9 %all_gather.69 = f32[256,128]{1,0:T(8,128)S(1)} all-gather(f32[16,128]{1,0:T(8,128)S(1)} %bitcast.256), channel_id=1, replica_groups=mesh['grp'=16,'row'=32] {'grp'}, dimensions={0}, use_global_device_ids=true | all-gather | bytes 139264 | tf_op jit(solution)/shard_map/all_gather | solution.py:80
  1578.1 16.4 all_gather.70
  1595.1 110.3 %psum.93 = f32[4,16,128]{2,1,0:T(8,128)S(1)} all-reduce(f32[4,16,128]{2,1,0:T(8,128)S(1)} %broadcast_multiply_fusion.4), channel_id=1, replica_groups=mesh['grp'=16,'row'=32] {'row'}, use_global_device_ids=true, to_apply=%region_15.16 | all-reduce | flops 8192 | bytes 65536 | tf_op jit(solution)/shard_map/psum | solution.py:79
  1705.5 41.9 %all_gather.71 = f32[256,128]{1,0:T(8,128)S(1)} all-gather(f32[16,128]{1,0:T(8,128)S(1)} %bitcast.254), channel_id=1, replica_groups=mesh['grp'=16,'row'=32] {'grp'}, dimensions={0}, use_global_device_ids=true | all-gather | bytes 139264 | tf_op jit(solution)/shard_map/all_gather | solution.py:80
  1747.6 16.4 all_gather.72
  1765.7 138.8 %all-reduce.9.cloned.1.call-done = f32[8,16,128]{2,1,0:T(8,128)} async-done(((f32[8,16,128]{2,1,0:T(8,128)}), f32[8,16,128]{2,1,0:T(8,128)}) %all-reduce.9.cloned.1.call-update) | async-done | bytes 65552 | tf_op jit(solution)/shard_map/psum | solution.py:79
  1905.4 22.9 %all_gather.73 = f32[256,128]{1,0:T(8,128)S(1)} all-gather(f32[16,128]{1,0:T(8,128)S(1)} %bitcast.250), channel_id=1, replica_groups=mesh['grp'=16,'row'=32] {'grp'}, dimensions={0}, use_global_device_ids=true | all-gather | bytes 139264 | tf_op jit(solution)/shard_map/all_gather | solution.py:80
  1928.6 15.1 all_gather.74
  1945.8 143.5 %all-reduce.11.cloned.1.call-done = f32[16,16,128]{2,1,0:T(8,128)} async-done(((f32[16,16,128]{2,1,0:T(8,128)}), f32[16,16,128]{2,1,0:T(8,128)}) %all-reduce.11.cloned.1.call-update) | async-done | bytes 131088 | tf_op jit(solution)/shard_map/psum | solution.py:79
  2090.5 22.7 %all_gather.75 = f32[256,128]{1,0:T(8,128)S(1)} all-gather(f32[16,128]{1,0:T(8,128)S(1)} %bitcast.251), channel_id=1, replica_groups=mesh['grp'=16,'row'=32] {'grp'}, dimensions={0}, use_global_device_ids=true | all-gather | bytes 139264 | tf_op jit(solution)/shard_map/all_gather | solution.py:80
  (89 shorter events, 21.4 us)
Async XLA Ops:
  7.2 1.9 copy-start
  7.2 68.3 %reduce-scatter.7.cloned.1.call-start = ((), (), s32[]{:S(2)}) async-start(), calls=%async_computation.6 | async-start | bytes 139264 | tf_op jit(solution)/shard_map/reduce_scatter | solution.py:51
  10.4 219.5 %copy-start.3 = (f32[1,16,128]{2,1,0:T(8,128)S(1)}, f32[1,16,128]{2,1,0:T(8,128)}, u32[]{:S(2)}) copy-start(f32[1,16,128]{2,1,0:T(8,128)} %param.11) | copy-start | bytes 24580
  10.4 242.2 %copy-start.1 = (f32[1,16,256]{2,1,0:T(8,128)S(1)}, f32[1,16,256]{2,1,0:T(8,128)}, u32[]{:S(2)}) copy-start(f32[1,16,256]{2,1,0:T(8,128)} %param.12) | copy-start | bytes 49156
  10.4 242.4 %copy-start.2 = (f32[1,6,16,256]{3,2,1,0:T(8,128)S(1)}, f32[1,6,16,256]{3,2,1,0:T(8,128)}, u32[]{:S(2)}) copy-start(f32[1,6,16,256]{3,2,1,0:T(8,128)} %param.13) | copy-start | bytes 294916
  13.4 215.4 %all-reduce.5.cloned.1.call-start = ((), (), s32[]{:S(2)}) async-start(), calls=%async_computation.7 | async-start | bytes 262144 | tf_op jit(solution)/shard_map/psum | solution.py:59
  77.0 229.1 %reduce-scatter.9.cloned.1.call-start = ((), (), s32[]{:S(2)}) async-start(), calls=%async_computation.8 | async-start | bytes 139264 | tf_op jit(solution)/shard_map/reduce_scatter | solution.py:51
  254.5 202.8 %all-reduce.7.cloned.1.call-start = ((), (), s32[]{:S(2)}) async-start(), calls=%async_computation.9 | async-start | bytes 131072 | tf_op jit(solution)/shard_map/psum | solution.py:59
  307.5 227.2 %reduce-scatter.11.cloned.1.call-start = ((), (), s32[]{:S(2)}) async-start(), calls=%async_computation.10 | async-start | bytes 139264 | tf_op jit(solution)/shard_map/reduce_scatter | solution.py:51
  483.1 264.6 %reduce-scatter.13.cloned.1.call-start = ((), (), s32[]{:S(2)}) async-start(), calls=%async_computation.11 | async-start | bytes 139264 | tf_op jit(solution)/shard_map/reduce_scatter | solution.py:51
  697.9 262.8 %reduce-scatter.15.cloned.1.call-start = ((), (), s32[]{:S(2)}) async-start(), calls=%async_computation.12 | async-start | bytes 139264 | tf_op jit(solution)/shard_map/reduce_scatter | solution.py:51
  910.9 195.5 %reduce-scatter.17.cloned.1.call-start = ((), (), s32[]{:S(2)}) async-start(), calls=%async_computation.13 | async-start | bytes 139264 | tf_op jit(solution)/shard_map/reduce_scatter | solution.py:51
  1056.6 847.8 %all-reduce.9.cloned.1.call-start = ((), (), s32[]{:S(2)}) async-start(), calls=%async_computation.14 | async-start | bytes 131072 | tf_op jit(solution)/shard_map/psum | solution.py:79
  1765.3 324.1 %all-reduce.11.cloned.1.call-start = ((), (), s32[]{:S(2)}) async-start(), calls=%async_computation.15 | async-start | bytes 262144 | tf_op jit(solution)/shard_map/psum | solution.py:79
Sparse Core Ops, SparseCore 0:
  13.5 61.9 reduce-scatter.6
  79.9 148.8 all-reduce.4
  254.6 51.4 reduce-scatter.8
  310.3 146.9 all-reduce.6
  483.2 51.4 reduce-scatter.10
  698.0 49.6 reduce-scatter.12
  911.0 49.5 reduce-scatter.14
  1056.7 49.5 reduce-scatter.16
  1765.4 139.0 all-reduce.8
  1945.6 143.7 all-reduce.10
where the time goes:
time: 2120 us
  blocking collectives  1190 us (56%)
  waiting for transfers between devices  881 us (42%)
  matrix products  24.7 us (1%)
    psum x4, blocking collectives, per_device(): update = pick_slot(lax.psum(placed, 'row'), picks)  353 us
    psum x4, blocking collectives, per_device(): ancestor = pick_slot(lax.psum(placed, 'row'), picks)  336 us
    psum x2, waiting for transfers between devices, per_device(): update = pick_slot(lax.psum(placed, 'row'), picks)  302 us
    reduce_scatter x6, waiting for transfers between devices, per_device(): lax.psum_scatter(upward(jnp.int32(0), share * lax.axis_size('grp')), 'grp...  297 us
    psum x2, waiting for transfers between devices, per_device(): ancestor = pick_slot(lax.psum(placed, 'row'), picks)  282 us
    all_gather x6, blocking collectives, per_device(): pending = lax.all_gather(inner_rhs[0] - update, 'grp', axis=0, tiled=True)  200 us
    all_gather x6, blocking collectives, per_device(): ancestor_full = lax.all_gather(ancestor, 'grp', axis=0, tiled=True)  187 us
    all_gather x6, blocking collectives, per_device(): rest = lax.all_gather(inner_fwd - inner_acc, 'grp', axis=0, tiled=True)  97.3 us
  transfers between devices with their start and end apart: 10, of which 10 were waited for; matrix products, arithmetic and copies ran while one was open for 0% of the time, Pallas kernels for 0%

commit v1 on v0

v1 whole, which is shorter than its diff:
```python
import functools

import jax
import jax.numpy as jnp
from jax import lax
from jax.experimental import pallas as pl
from jax.experimental.pallas import tpu as pltpu
from jax.sharding import PartitionSpec as P

F32 = jnp.float32
BF16 = jnp.bfloat16
NN = (((1,), (0,)), ((), ()))
NT = (((1,), (1,)), ((), ()))


def split(x):
    high = x.astype(BF16)
    return high, (x - high.astype(F32)).astype(BF16)


def dot(a, b, dims):
    return lax.dot_general(a, b, dims, preferred_element_type=F32)


def product(a, b, dims=NN):
    return dot(a[0], b[0], dims) + (dot(a[0], b[1], dims) + dot(a[1], b[0], dims))


def thin(x, w, dims):
    rows = x.shape[0]
    high = x.astype(BF16).astype(F32)
    both = jnp.concatenate([high, x - high], axis=0).astype(BF16)
    first, second = dot(both, w[0], dims), dot(both, w[1], dims)
    return first[:rows] + (first[rows:] + second[:rows])


def kernel(
    chips, count,
    rhs_h, inv_h, pan_h, mask_s, irhs_h, iinv_h, ipan_h,
    leaf_out, inner_out,
    v_rhs, v_inv, v_pan, i_hi, i_lo, p_hi, p_lo, leaf_t,
    terms, terms_in, pieces, upd,
    blocks, rblock, rhs_t, b_hi, b_lo,
    child_in, lat_in, pend, fwd, acc, sol, full, leaf_acc, turned,
    in_sem, own_sem, ring_recv, ring_send, sib_recv, sib_send,
    t_recv, t_send, a_recv, a_send, lat_recv, lat_send,
    up_recv, up_send, down_recv, down_send,
    ag_recv, ag_send, pair_recv, pair_send,
):
    top = pan_h.shape[0]
    width, nrhs = v_rhs.shape
    member = lax.axis_index("grp")
    j = lax.axis_index("row")
    z, c = lax.div(member, 2), lax.rem(member, 2)
    other = 1 - c
    lev, low = jnp.int32(1), jnp.int32(1)
    for bit in range(1, top):
        even = (lax.rem(j, 2**bit) == 0).astype(jnp.int32)
        lev, low = lev + even, low * (1 + even)
    is_top = lev == top
    has_child = lev >= 2
    two_children = jnp.logical_and(has_child, lev < top)
    parent = lax.div(j, low * 4) * low * 4 + low * 2
    parent = jnp.where(lev == top - 1, 0, parent)
    slot = lax.rem(lax.div(j, low * 2), 2)
    child0 = lax.rem(j - lax.div(low, 2) + count, count)
    child1 = lax.rem(j + lax.div(low, 2), count)
    above = lax.rem(j - low + count, count)

    def at(zz=None, cc=None, jj=None):
        zz = z if zz is None else zz
        cc = c if cc is None else cc
        return {"grp": zz * 2 + cc, "row": j if jj is None else jj}

    def turn(step):
        return lax.rem(z + step + chips, chips)

    def remote(src, dst, send, recv, where):
        return pltpu.make_async_remote_copy(
            src_ref=src, dst_ref=dst, send_sem=send, recv_sem=recv,
            device_id=where, device_id_type=pl.DeviceIdType.MESH,
        )

    def await_bytes(ref, sem):
        pltpu.make_async_copy(ref, ref, sem).wait()

    def local(src, dst, sem):
        return pltpu.make_async_copy(src, dst, sem)

    def own_copies(b):
        return local(ipan_h.at[b], blocks.at[b, z, c], own_sem.at[b])

    local(rhs_h, v_rhs, in_sem.at[top]).start()
    local(inv_h, v_inv, in_sem.at[top + 1]).start()
    own_inv = local(iinv_h, blocks.at[0, z, c], own_sem.at[0])
    own_rhs = local(irhs_h, rblock.at[z, c], own_sem.at[top])
    own_inv.start()
    own_rhs.start()

    @pl.loop(lev, top)
    def _(b):
        own_copies(b).start()

    for step in range(top):
        local(pan_h.at[step], v_pan.at[step], in_sem.at[step]).start()

    barrier = pltpu.get_barrier_semaphore()

    def greet(where):
        pl.semaphore_signal(barrier, inc=1, device_id=where, device_id_type=pl.DeviceIdType.MESH)

    greet(at(cc=other))
    for step in range(1, chips):
        greet(at(zz=turn(step)))

    @pl.when(lev < top)
    def _():
        greet(at(jj=parent))
        greet(at(jj=above))

    @pl.when(has_child)
    def _():
        greet(at(jj=child0))

    @pl.when(two_children)
    def _():
        greet(at(jj=child1))

    for level in range(1, top):
        @pl.when(lev > level)
        def _(level=level):
            greet(at(jj=lax.rem(j + 2 ** (level - 1), count)))

    expected = chips + (lev - 1) + has_child.astype(jnp.int32)
    expected = expected + two_children.astype(jnp.int32) + 2 * (lev < top).astype(jnp.int32)
    pl.semaphore_wait(barrier, expected)

    right, left = chips // 2, chips - 1 - chips // 2

    def shard(b, zz):
        return rblock.at[zz, c] if b is None else blocks.at[b, zz, c]

    def sem_of(b):
        return top if b is None else b

    def ring(b, way, step):
        src = turn(-step if way == 0 else step)
        ref = shard(b, src)
        target = turn(1 if way == 0 else -1)
        i = sem_of(b)
        return remote(ref, ref, ring_send.at[i], ring_recv.at[way, step, i], at(zz=target))

    def ring_arrived(b, way, step):
        src = turn(-step - 1 if way == 0 else step + 1)
        await_bytes(shard(b, src), ring_recv.at[way, step, sem_of(b)])

    def each_block(body):
        body(0)
        body(None)
        pl.loop(lev, top)(body)

    def first_step(b):
        if b is None:
            own_rhs.wait()
        elif isinstance(b, int):
            own_inv.wait()
        else:
            own_copies(b).wait()
        if right:
            ring(b, 0, 0).start()
        if left:
            ring(b, 1, 0).start()

    each_block(first_step)

    def next_step(step):
        def body(b):
            if step <= right:
                ring_arrived(b, 0, step - 1)
                if step < right:
                    ring(b, 0, step).start()
            if step <= left:
                ring_arrived(b, 1, step - 1)
                if step < left:
                    ring(b, 1, step).start()
        each_block(body)

    local(rhs_h, v_rhs, in_sem.at[top]).wait()
    local(inv_h, v_inv, in_sem.at[top + 1]).wait()
    hi, lo = split(v_inv[...])
    i_hi[...] = hi
    i_lo[...] = lo
    forward = product((hi, lo), split(v_rhs[...])).T
    leaf_t[...] = forward
    forward = split(forward)

    @pl.loop(0, top)
    def _(step):
        local(pan_h.at[step], v_pan.at[step], in_sem.at[step]).wait()
        hi, lo = split(v_pan[step])
        p_hi[step] = hi
        p_lo[step] = lo
        term = product(forward, (hi, lo)) * mask_s[step].astype(F32)
        terms[:, :, step] = term.reshape(2, chips, -1, width)
        remote(
            terms.at[other, :, step], terms_in.at[:, step],
            t_send, t_recv.at[step], at(cc=other),
        ).start()

    groups = [(0, 1), (1, top)]
    for number, (first, last) in enumerate(groups):
        @pl.loop(first, last)
        def _(step):
            await_bytes(terms_in.at[:, step], t_recv.at[step])
            terms[c, :, step] = terms[c, :, step] + terms_in[:, step]

        for step in range(1, chips):
            zz = turn(step)
            remote(
                terms.at[c, zz, first:last], pieces.at[z, first:last],
                a_send, a_recv.at[number], at(zz=zz),
            ).start()

    for step in range(1, max(right, left) + 1):
        next_step(step)

    def share_block(b):
        ref = rblock.at[:, c] if b is None else blocks.at[b, :, c]
        i = sem_of(b)
        remote(ref, ref, sib_send.at[i], sib_recv.at[i], at(cc=other)).start()

    each_block(share_block)

    for number, (first, last) in enumerate(groups):
        if chips > 1:
            await_bytes(pieces.at[0 : chips - 1, first:last], a_recv.at[number])
        total = terms[c, z, first:last]
        for step in range(1, chips):
            total = total + pieces[turn(step), first:last]
        upd[first:last] = total

    def lateral_up(level):
        l = level - 1
        return remote(
            upd.at[l], lat_in, lat_send.at[l], lat_recv,
            at(jj=lax.rem(j + 2**l, count)),
        )

    for level in range(1, top):
        @pl.when(lev > level)
        def _(level=level):
            lateral_up(level).start()

    def take_block(b):
        if b is None:
            await_bytes(rblock.at[:, other], sib_recv.at[top])
            rhs_t[...] = rblock[...].reshape(width, nrhs).T.reshape(rhs_t.shape)
        else:
            await_bytes(blocks.at[b, :, other], sib_recv.at[b])
            hi, lo = split(blocks[b].reshape(width, width))
            b_hi[b] = hi
            b_lo[b] = lo

    each_block(take_block)

    own = lev - 1
    pend[...] = rhs_t[c, z] - upd[own]

    @pl.when(has_child)
    def _():
        await_bytes(child_in.at[0, own], up_recv.at[0, own])
        pend[...] = pend[...] - child_in[0, own]

    @pl.when(two_children)
    def _():
        await_bytes(child_in.at[1, own], up_recv.at[1, own])
        pend[...] = pend[...] - child_in[1, own]

    @pl.when(lev < top)
    def _():
        await_bytes(lat_in, lat_recv)
        pend[...] = pend[...] - lat_in[...]

    fwd[...] = thin(pend[...], (b_hi[0], b_lo[0]), NT)

    def send_up(l):
        return remote(
            upd.at[l], child_in.at[slot, l], up_send.at[l], up_recv.at[slot, l], at(jj=parent)
        )

    @pl.loop(lev, top)
    def _(l):
        upd[l] = upd[l] + thin(fwd[...], (b_hi[l], b_lo[l]), NN)

        @pl.when(has_child)
        def _():
            await_bytes(child_in.at[0, l], up_recv.at[0, l])
            await_bytes(child_in.at[1, l], up_recv.at[1, l])
            upd[l] = upd[l] + child_in[0, l] + child_in[1, l]

        send_up(l).start()

    acc[...] = jnp.zeros_like(acc)
    leaf_acc[...] = jnp.zeros_like(leaf_acc)

    def send_down(l, which):
        target = (child0, child1, above)[which]
        return remote(
            sol.at[l], sol.at[l], down_send.at[which, l], down_recv.at[l], at(jj=target)
        )

    def spread(l, step):
        zz = turn(step)
        return remote(sol.at[l], full.at[l, c, z], ag_send.at[l], ag_recv.at[l], at(zz=zz))

    def pair(l):
        return remote(full.at[l, c], full.at[l, c], pair_send.at[l], pair_recv.at[l], at(cc=other))

    def descend(l):
        @pl.when(l + 1 > lev)
        def _():
            await_bytes(sol.at[l], down_recv.at[l])

            @pl.when(has_child)
            def _():
                send_down(l, 0).start()
                send_down(l, 1).start()

            acc[...] = acc[...] + thin(sol[l], (b_hi[l], b_lo[l]), NT)

        @pl.when(l + 1 == lev)
        def _():
            sol[l] = thin(fwd[...] - acc[...], (b_hi[0], b_lo[0]), NN)

            @pl.when(has_child)
            def _():
                send_down(l, 0).start()

            @pl.when(two_children)
            def _():
                send_down(l, 1).start()

            @pl.when(lev < top)
            def _():
                send_down(l, 2).start()

        @pl.when(l + 1 < lev)
        def _():
            await_bytes(sol.at[l], down_recv.at[l])

        for step in range(1, chips):
            spread(l, step).start()
        full[l, c, z] = sol[l]

    def join(l):
        if chips > 1:
            await_bytes(full.at[l, c, 0 : chips - 1], ag_recv.at[l])
        pair(l).start()

    def leaf_back(l):
        await_bytes(full.at[l, other], pair_recv.at[l])
        ancestor = split(full[l].reshape(nrhs, width))
        leaf_acc[...] = leaf_acc[...] + mask_s[l].astype(F32) * product(
            ancestor, (p_hi[l], p_lo[l]), NT
        )

    @pl.loop(0, top + 2)
    def _(i):
        l = top - 1 - i

        @pl.when(i < top)
        def _():
            descend(l)

        @pl.when(jnp.logical_and(i >= 1, i < top + 1))
        def _():
            join(l + 1)

        @pl.when(i >= 2)
        def _():
            leaf_back(l + 2)

    rest = split(leaf_t[...] - leaf_acc[...])
    leaf_out[...] = product(rest, (i_hi[...], i_lo[...])).T
    share = inner_out.shape[0]
    turned[...] = full[own].reshape(nrhs, width).T
    inner_out[...] = turned[pl.ds(pl.multiple_of(member * share, share), share), :]

    def sent_block(b):
        i = sem_of(b)
        if chips > 1:
            ref = rblock.at[0 : chips - 1, 0] if b is None else blocks.at[b, 0 : chips - 1, 0]
            await_bytes(ref, ring_send.at[i])
        ref = rblock.at[:, c] if b is None else blocks.at[b, :, c]
        await_bytes(ref, sib_send.at[i])

    each_block(sent_block)
    await_bytes(terms.at[0], t_send)
    if chips > 1:
        await_bytes(terms.at[0, 0 : chips - 1], a_send)
    for level in range(1, top):
        @pl.when(lev > level)
        def _(level=level):
            lateral_up(level).wait_send()

    @pl.loop(lev, top)
    def _(l):
        send_up(l).wait_send()

    @pl.loop(own, top)
    def _(l):
        @pl.when(has_child)
        def _():
            send_down(l, 0).wait_send()

        @pl.when(two_children)
        def _():
            send_down(l, 1).wait_send()

    @pl.when(lev < top)
    def _():
        send_down(own, 2).wait_send()

    @pl.loop(0, top)
    def _(l):
        if chips > 1:
            await_bytes(full.at[l, 0, 0 : chips - 1], ag_send.at[l])
        pair(l).wait_send()


def per_device(leaf_rhs, leaf_inv, leaf_panel, leaf_mask, inner_rhs, inner_inv, inner_panel):
    members, count = lax.axis_size("grp"), lax.axis_size("row")
    chips = members // 2
    width, nrhs = leaf_rhs.shape[2:]
    top = leaf_panel.shape[2]
    share, cols = width // members, nrhs // members
    hbm = pl.BlockSpec(memory_space=pl.ANY)
    dma = pltpu.SemaphoreType.DMA
    steps = max(chips // 2, 1)
    v = pltpu.VMEM
    call = pl.pallas_call(
        functools.partial(kernel, chips, count),
        out_shape=(
            jax.ShapeDtypeStruct((width, nrhs), F32),
            jax.ShapeDtypeStruct((share, nrhs), F32),
        ),
        in_specs=[hbm, hbm, hbm, pl.BlockSpec(memory_space=pltpu.SMEM), hbm, hbm, hbm],
        out_specs=[pl.BlockSpec(memory_space=pltpu.VMEM)] * 2,
        scratch_shapes=[
            v((width, nrhs), F32),
            v((width, width), F32),
            v((top, width, width), F32),
            v((width, width), BF16),
            v((width, width), BF16),
            v((top, width, width), BF16),
            v((top, width, width), BF16),
            v((nrhs, width), F32),
            v((2, chips, top, cols, width), F32),
            v((chips, top, cols, width), F32),
            v((chips, top, cols, width), F32),
            v((top, cols, width), F32),
            v((top, chips, 2, share, width), F32),
            v((chips, 2, share, nrhs), F32),
            v((2, chips, cols, width), F32),
            v((top, width, width), BF16),
            v((top, width, width), BF16),
            v((2, top, cols, width), F32),
            v((cols, width), F32),
            v((cols, width), F32),
            v((cols, width), F32),
            v((cols, width), F32),
            v((top, cols, width), F32),
            v((top, 2, chips, cols, width), F32),
            v((nrhs, width), F32),
            v((width, nrhs), F32),
            dma((top + 2,)),
            dma((top + 1,)),
            dma((2, steps, top + 1)),
            dma((top + 1,)),
            dma((top + 1,)),
            dma((top + 1,)),
            dma((top,)),
            dma,
            dma((2,)),
            dma,
            dma,
            dma((top,)),
            dma((2, top)),
            dma((top,)),
            dma((top,)),
            dma((3, top)),
            dma((top,)),
            dma((top,)),
            dma((top,)),
            dma((top,)),
        ],
        compiler_params=pltpu.CompilerParams(
            collective_id=0, has_side_effects=True, vmem_limit_bytes=48 * 2**20
        ),
    )
    leaf, inner = call(
        leaf_rhs[0, 0], leaf_inv[0, 0], leaf_panel[0, 0], leaf_mask[0, 0],
        inner_rhs[0], inner_inv[0], inner_panel[0],
    )
    return leaf[None, None], inner[None]


def solution(mesh):
    in_specs = (
        P("row", "grp", None, None),
        P("row", "grp", None, None),
        P("row", "grp", None, None, None),
        P("row", "grp", None),
        P("row", "grp", None),
        P("row", "grp", None),
        P("row", None, "grp", None),
    )
    out_specs = (P("row", "grp", None, None), P("row", "grp", None))
    return jax.shard_map(
        per_device, mesh=mesh, in_specs=in_specs, out_specs=out_specs, check_vma=False
    )
```

time: 2120 us -> 110 us (0.05)
  blocking collectives: 1190 us -> 0 us
  waiting for transfers between devices: 881 us -> 0 us
  Pallas kernels: 0 us -> 101 us
  matrix products: 24.7 us -> 0 us
    psum x8 -> x0, blocking collectives: 689 us -> none  [the longest x4 353 us: per_device(): update = pick_slot(lax.psum(placed, 'row'), picks)]
    psum x4 -> x0, waiting for transfers between devices: 584 us -> none  [the longest x2 302 us: per_device(): update = pick_slot(lax.psum(placed, 'row'), picks)]
    all_gather x19 -> x0, blocking collectives: 501 us -> none  [the longest x6 200 us: per_device(): pending = lax.all_gather(inner_rhs[0] - update, 'grp', axis=0, tiled=True)]
    reduce_scatter x6 -> x0, waiting for transfers between devices: 297 us -> none  [per_device(): lax.psum_scatter(upward(jnp.int32(0), share * lax.axis_size('grp')), 'grp...]
    pallas_call x0 -> x1, Pallas kernels: none -> 101 us  [per_device(): call(leaf_rhs[0, 0], leaf_inv[0, 0], leaf_panel[0, 0], leaf_mask[0, 0], i...]
    dot_general x45 -> x0, matrix products: 24.7 us -> none  [the longest x6 7.51 us: upward(): jnp.einsum('lna,lnr->ar', masked_now, leaf_fwd, precision=highest)]
  transfers between devices with their start and end apart: 10 -> 0, of which waited for: 10 -> 0; matrix products, arithmetic and copies ran while one was open for 0% -> 0% of each run, Pallas kernels for 0% -> 0%
where the time goes in v1:
time: 110 us; the launch traced here: 109 us
  Pallas kernels  101 us (92%)
  local copies, waits for them, and re-layouts  7.47 us (7%)
    pallas_call x1, Pallas kernels, per_device(): call(leaf_rhs[0, 0], leaf_inv[0, 0], leaf_panel[0, 0], leaf_mask[0, 0], i...  101 us
    unnamed x16, local copies, waits for them, and re-layouts  7.47 us

profile of v1, /device:TPU:1, one launch (start us, length us, event | category | flops | bytes accessed | tf_op | source)
XLA Modules:
  0.0 109.3 jit_solution(12465548991488911075)
XLA Ops:
  0.6 0.0 copy-start
  0.6 1.4 %copy-done = f32[1,1,6,256,256]{4,3,2,1,0:T(8,128)S(1)} copy-done((f32[1,1,6,256,256]{4,3,2,1,0:T(8,128)S(1)}, f32[1,1,6,256,256]{4,3,2,1,0:T(8,128)}, u32[]{:S(2)}) %copy-start) | copy-done | bytes 1572888
  2.0 0.0 copy-start.1
  2.0 0.9 copy-done.1
  3.0 0.0 copy-start.2
  3.0 0.9 copy-done.2
  3.9 0.0 copy-start.3
  3.9 0.9 copy-done.3
  4.8 0.0 copy-start.4
  4.8 0.7 copy-done.4
  5.5 0.0 copy-start.5
  5.5 0.7 copy-done.5
  6.2 0.0 copy-start.6
  6.2 0.7 copy-done.6
  6.9 101.2 %shard_map.86 = (f32[256,128]{1,0:T(8,128)S(1)}, f32[16,128]{1,0:T(8,128)S(1)}) custom-call(f32[256,128]{1,0:T(8,128)S(1)} %bitcast.11, f32[256,256]{1,0:T(8,128)S(1)} %bitcast.10, f32[6,256,256]{2,1,0:T(8,128)S(1)} %bitcast.9, s32[6]{0:T(128)S(1)} %bitcast.17, f32[16,128]{1,0:T(8,128)S(1)} %bitcast.15, f32[16,256]{1,0:T(8,128)S(1)} %bitcast.14, ...), custom_call_target="tpu_custom_call" | custom-call | tf_op jit(solution)/shard_map/pallas_call | solution.py:501
  108.1 0.7 copy.11
  108.7 0.6 copy.12
Async XLA Ops:
  0.6 1.4 %copy-start = (f32[1,1,6,256,256]{4,3,2,1,0:T(8,128)S(1)}, f32[1,1,6,256,256]{4,3,2,1,0:T(8,128)}, u32[]{:S(2)}) copy-start(f32[1,1,6,256,256]{4,3,2,1,0:T(8,128)} %param.9) | copy-start | bytes 4718596
  2.0 0.9 copy-start.1
  3.0 0.9 copy-start.2
  3.9 0.9 copy-start.3
  4.8 0.7 copy-start.4
  5.5 0.7 copy-start.5
  6.2 0.7 copy-start.6

commit v2 on v0

v2 whole, which is shorter than its diff:
```python
import functools

import jax
import jax.numpy as jnp
from jax import lax
from jax.experimental import pallas as pl
from jax.experimental.pallas import tpu as pltpu
from jax.sharding import PartitionSpec as P

F32 = jnp.float32
BF16 = jnp.bfloat16
NN = (((1,), (0,)), ((), ()))
NT = (((1,), (1,)), ((), ()))
EIGHT = 8


def split(x):
    high = x.astype(BF16)
    return high, (x - high.astype(F32)).astype(BF16)


def dot(a, b, dims):
    return lax.dot_general(a, b, dims, preferred_element_type=F32)


def product(a, b, dims=NN):
    return dot(a[0], b[0], dims) + (dot(a[0], b[1], dims) + dot(a[1], b[0], dims))


def thin(x, w, dims):
    rows = x.shape[0]
    high = x.astype(BF16).astype(F32)
    both = jnp.concatenate([high, x - high], axis=0).astype(BF16)
    first, second = dot(both, w[0], dims), dot(both, w[1], dims)
    return first[:rows] + (first[rows:] + second[:rows])


class Plan:
    def __init__(self, top, count):
        self.groups = count // EIGHT
        self.host3 = 14 if count > EIGHT else 6
        order = [(2, 0)] + [(2, l) for l in range(3, top + 1)] + [(6, 0), (6, 3), (4, 0)]
        for l in range(4, top + 1):
            order += [(6, l), (4, l)]
        self.mid = {key: i for i, key in enumerate(order)}
        self.mid_local = top - 1
        self.mid_rhs = {2: 0, 6: 1, 4: 2}
        self.nodes = []
        for l in range(4, top):
            self.nodes += [(l, a) for a in range(2 ** (l - 1), count, 2**l)]
        self.nodes.append((top, 0))
        self.covers = {}
        for l, a in self.nodes:
            first = 0 if l == top else a - 2 ** (l - 1)
            last = count if l == top else a + 2 ** (l - 1)
            self.covers[a] = (first // EIGHT, last // EIGHT)
        self.below = {
            a: [d for k, d in self.nodes if k < l
                and self.covers[a][0] <= self.covers[d][0] < self.covers[a][1]]
            for l, a in self.nodes
        }
        order = []
        for l, a in self.nodes:
            order += [(d, l) for d in self.below[a]] + [(a, 0)]
        self.high = {key: i for i, key in enumerate(order)}
        self.high_rhs = {a: i for i, (l, a) in enumerate(self.nodes)}
        self.blocks = max(top, len(self.mid), len(self.high))
        self.rhs = max(3, len(self.nodes))


def kernel(
    chips, count, plan,
    rhs_h, inv_h, pan_h, mask_s, irhs_h, iinv_h, ipan_h,
    leaf_out, inner_out,
    v_rhs, v_inv, v_pan, i_hi, i_lo, p_hi, p_lo, leaf_t,
    terms, terms_in, pieces1, pieces, upd,
    blocks, rblock, rhs_t, b_hi, b_lo,
    vin, win, wout, fwd, sol, solb, xhigh, full, leaf_acc, turned,
    in_sem, arr_sem, arr_rhs, put_send,
    ring_recv, ring_send, rring_recv, rring_send, sib_recv, sib_send, rsib_recv, rsib_send,
    t_recv, t_send, a1_recv, a1_send, a_recv, a_send,
    v_recv, v_send, w_recv, w_send, x_send, down_recv, down_send,
    ag_recv, ag_send, left_send, pair_recv, pair_send,
):
    top = pan_h.shape[0]
    width, nrhs = v_rhs.shape
    member = lax.axis_index("grp")
    j = lax.axis_index("row")
    z, c = lax.div(member, 2), lax.rem(member, 2)
    other = 1 - c
    parity = lax.rem(j, 2)
    place = lax.rem(j, EIGHT)
    group = lax.div(j, EIGHT)
    start = j - place
    host2 = start + 2
    odd, even = parity == 1, parity == 0
    is2 = place == 2
    is3 = j == plan.host3
    mate = jnp.where(odd, j - 1, j + 1)
    lev = jnp.int32(1)
    for bit in range(1, top):
        lev = lev + (lax.rem(j, 2**bit) == 0).astype(jnp.int32)
    nblocks = jnp.where(odd, top, jnp.where(is2, len(plan.mid), jnp.where(is3, len(plan.high), 0)))
    nlocal = jnp.where(odd, top, jnp.where(is2, plan.mid_local, 0))
    nnodes = jnp.where(odd, 1, jnp.where(is2, 3, jnp.where(is3, len(plan.nodes), 0)))
    nlocal_rhs = jnp.where(jnp.logical_or(odd, is2), 1, 0)

    def at(zz=None, cc=None, jj=None):
        zz = z if zz is None else zz
        cc = c if cc is None else cc
        return {"grp": zz * 2 + cc, "row": j if jj is None else jj}

    def turn(step):
        return lax.rem(z + step + chips, chips)

    def remote(src, dst, send, recv, where):
        return pltpu.make_async_remote_copy(
            src_ref=src, dst_ref=dst, send_sem=send, recv_sem=recv,
            device_id=where, device_id_type=pl.DeviceIdType.MESH,
        )

    def local(src, dst, sem):
        return pltpu.make_async_copy(src, dst, sem)

    def await_bytes(ref, sem):
        pltpu.make_async_copy(ref, ref, sem).wait()

    rhs_in = local(rhs_h, v_rhs, in_sem.at[top])
    inv_in = local(inv_h, v_inv, in_sem.at[top + 1])
    rhs_in.start()
    inv_in.start()

    def panel_in(step):
        return local(pan_h.at[step], v_pan.at[step], in_sem.at[step])

    panel_in(0).start()

    def keep(l, slot):
        src = iinv_h if l == 0 else ipan_h.at[l - 1]
        local(src, blocks.at[slot, z, c], arr_sem.at[slot]).start()

    @pl.when(odd)
    def _():
        for l in [0] + list(range(2, top + 1)):
            keep(l, max(l - 1, 0))

    @pl.when(is2)
    def _():
        for l in [0] + list(range(3, top + 1)):
            keep(l, plan.mid[2, l])

    @pl.when(jnp.logical_or(odd, is2))
    def _():
        local(irhs_h, rblock.at[0, z, c], arr_rhs.at[0]).start()

    for step in range(1, top):
        panel_in(step).start()

    barrier = pltpu.get_barrier_semaphore()

    def greet(where):
        pl.semaphore_signal(barrier, inc=1, device_id=where, device_id_type=pl.DeviceIdType.MESH)

    greet(at(cc=other))
    for step in range(1, chips):
        greet(at(zz=turn(step)))
    for step in range(chips):
        greet(at(zz=turn(step), jj=mate))

    @pl.when(is2)
    def _():
        for r in range(EIGHT):
            if r != 2:
                greet(at(jj=start + r))
        greet(at(jj=plan.host3))

    @pl.when(jnp.logical_not(is2))
    def _():
        greet(at(jj=host2))

    @pl.when(is3)
    def _():
        for g in range(plan.groups):
            greet(at(jj=g * EIGHT + 2))
        for l, a in plan.nodes:
            greet(at(jj=a))

    @pl.when(place == 0)
    def _():
        greet(at(jj=plan.host3))

    expected = 2 * chips + jnp.where(is2, EIGHT, 1)
    expected = expected + jnp.where(is3, plan.groups + len(plan.nodes), 0)
    expected = expected + jnp.where(place == 0, 1, 0)
    pl.semaphore_wait(barrier, expected)

    def puts(slots, rhs_slots, key, levels, target):
        for n, l in enumerate([0] + levels):
            src = iinv_h if l == 0 else ipan_h.at[l - 1]
            slot = slots[key, l]
            yield remote(
                src, blocks.at[slot, z, c], put_send.at[n], arr_sem.at[slot], at(jj=target)
            )
        slot = rhs_slots[key]
        yield remote(
            irhs_h, rblock.at[slot, z, c], put_send.at[top], arr_rhs.at[slot], at(jj=target)
        )

    def each_put(act):
        for key, l in ((6, 2), (4, 3)):
            @pl.when(place == key)
            def _(key=key, l=l):
                levels = list(range(l + 1, top + 1))
                for copy in puts(plan.mid, plan.mid_rhs, key, levels, host2):
                    act(copy)
        for l, a in plan.nodes:
            @pl.when(j == a)
            def _(l=l, a=a):
                levels = list(range(l + 1, top + 1))
                for copy in puts(plan.high, plan.high_rhs, a, levels, plan.host3):
                    act(copy)

    each_put(lambda copy: copy.start())

    right, left = chips // 2, chips - 1 - chips // 2

    def ring(buffer, send, recv, way, step, b):
        src = turn(-step if way == 0 else step)
        ref = buffer.at[b, src, c]
        target = turn(1 if way == 0 else -1)
        return remote(ref, ref, send.at[b], recv.at[way, step, b], at(zz=target))

    def ring_arrived(buffer, recv, way, step, b):
        src = turn(-step - 1 if way == 0 else step + 1)
        await_bytes(buffer.at[b, src, c], recv.at[way, step, b])

    kinds = (
        (blocks, arr_sem, ring_send, ring_recv, sib_send, sib_recv, nlocal, nblocks),
        (rblock, arr_rhs, rring_send, rring_recv, rsib_send, rsib_recv, nlocal_rhs, nnodes),
    )

    def first_step(near):
        for buffer, arrived, send, recv, _, _, mine, every in kinds:
            @pl.loop(0 if near else mine, mine if near else every)
            def _(b):
                await_bytes(buffer.at[b, z, c], arrived.at[b])
                if right:
                    ring(buffer, send, recv, 0, 0, b).start()
                if left:
                    ring(buffer, send, recv, 1, 0, b).start()

    def next_step(step):
        for buffer, _, send, recv, give, got, _, every in kinds:
            @pl.loop(0, every)
            def _(b):
                if step <= right:
                    ring_arrived(buffer, recv, 0, step - 1, b)
                    if step < right:
                        ring(buffer, send, recv, 0, step, b).start()
                if step <= left:
                    ring_arrived(buffer, recv, 1, step - 1, b)
                    if step < left:
                        ring(buffer, send, recv, 1, step, b).start()
                if step == max(right, left):
                    share(buffer, give, got, b).start()

    def share(buffer, send, recv, b):
        ref = buffer.at[b, :, c]
        return remote(ref, ref, send.at[b], recv.at[b], at(cc=other))

    def take_rhs(b):
        await_bytes(rblock.at[b, :, other], rsib_recv.at[b])
        rhs_t[b] = rblock[b].reshape(width, nrhs).T.reshape(rhs_t.shape[1:])

    def take_block(b):
        await_bytes(blocks.at[b, :, other], sib_recv.at[b])
        hi, lo = split(blocks[b].reshape(width, width))
        b_hi[b] = hi
        b_lo[b] = lo

    def block(b):
        return b_hi[b], b_lo[b]

    first_step(True)

    rhs_in.wait()
    inv_in.wait()
    hi, lo = split(v_inv[...])
    i_hi[...] = hi
    i_lo[...] = lo
    forward = product((hi, lo), split(v_rhs[...])).T
    leaf_t[...] = forward
    forward = split(forward)

    def swap_cores(l):
        return remote(
            terms.at[other, :, l], terms_in.at[:, l], t_send, t_recv.at[l], at(cc=other)
        )

    @pl.loop(0, top)
    def _(l):
        panel_in(l).wait()
        hi, lo = split(v_pan[l])
        p_hi[l] = hi
        p_lo[l] = lo
        term = product(forward, (hi, lo)) * mask_s[l].astype(F32)
        terms[:, :, l] = term.reshape(2, chips, -1, width)
        swap_cores(l).start()

    def add_cores(l):
        await_bytes(terms_in.at[:, l], t_recv.at[l])
        terms[c, :, l] = terms[c, :, l] + terms_in[:, l]

    def send_first(step):
        return remote(
            terms.at[c, turn(step), 0], pieces1.at[parity, z],
            a1_send.at[0 if step else 1], a1_recv.at[parity], at(zz=turn(step), jj=jnp.where(odd, j, mate)),
        )

    add_cores(0)

    @pl.when(even)
    def _():
        send_first(0).start()

    for step in range(1, chips):
        send_first(step).start()

    pl.loop(1, top)(add_cores)
    for step in range(1, chips):
        remote(
            terms.at[c, turn(step), 1:top], pieces.at[z], a_send, a_recv, at(zz=turn(step))
        ).start()

    first_step(False)
    for step in range(1, max(right, left)):
        next_step(step)

    @pl.when(odd)
    def _():
        next_step(max(right, left))

    def own_sum():
        await_bytes(pieces.at[0 : chips - 1], a_recv)
        total = terms[c, z, 1:top]
        for step in range(1, chips):
            total = total + pieces[turn(step)]
        upd[...] = total

    def send_v(l):
        return remote(
            upd.at[l - 2], vin.at[l - 2, place], v_send.at[l - 2], v_recv.at[l - 2], at(jj=host2)
        )

    @pl.when(even)
    def _():
        own_sum()

        @pl.when(is2)
        def _():
            vin[:, 2] = upd[...]

        @pl.when(jnp.logical_not(is2))
        def _():
            for l in range(2, top + 1):
                send_v(l).start()

        next_step(max(right, left))

    @pl.when(odd)
    def _():
        take_rhs(0)
        take_block(0)
        await_bytes(pieces1.at[0], a1_recv.at[0])
        await_bytes(pieces1.at[0, 0 : chips - 1], a1_recv.at[1])
        total = terms[c, z, 0] + pieces1[0, z]
        for step in range(1, chips):
            total = total + (pieces1[0, turn(step)] + pieces1[1, turn(step)])
        fwd[0] = thin(rhs_t[0, c, z] - total, block(0), NT)
        own_sum()

        @pl.loop(2, top + 1)
        def _(l):
            take_block(l - 1)
            upd[l - 2] = upd[l - 2] + thin(fwd[0], block(l - 1), NN)
            send_v(l).start()

    mid = plan.mid
    order = (1, 3, 5, 7, 0, 4, 6)

    def send_w(l):
        return remote(
            wout.at[l - 4], win.at[l - 4, group], w_send.at[l - 4], w_recv.at[l - 4],
            at(jj=plan.host3),
        )

    def arrived(l):
        await_bytes(vin.at[l - 2, 0 : EIGHT - 1], v_recv.at[l - 2])

    def slots(l, first, last):
        total = vin[l - 2, first]
        for r in range(first + 1, last):
            total = total + vin[l - 2, r]
        return total

    @pl.when(is2)
    def _():
        for b in range(3):
            take_rhs(b)
        pl.loop(0, len(mid))(take_block)
        arrived(2)
        fwd[0] = thin(rhs_t[0, c, z] - slots(2, 0, 4), block(mid[2, 0]), NT)
        fwd[1] = thin(rhs_t[1, c, z] - slots(2, 4, 8), block(mid[6, 0]), NT)
        arrived(3)
        fwd[2] = thin(
            rhs_t[2, c, z] - slots(3, 0, 8) - thin(fwd[0], block(mid[2, 3]), NN)
            - thin(fwd[1], block(mid[6, 3]), NN),
            block(mid[4, 0]), NT,
        )
        for l in range(4, top + 1):
            arrived(l)
            wout[l - 4] = slots(l, 0, 8) + (
                thin(fwd[0], block(mid[2, l]), NN) + thin(fwd[1], block(mid[6, l]), NN)
            ) + thin(fwd[2], block(mid[4, l]), NN)
            send_w(l).start()

    level_of = {a: l for l, a in plan.nodes}

    def send_x(a, g):
        n = plan.high_rhs[a]
        l = level_of[a]
        return remote(
            xhigh.at[n], sol.at[l - 1], x_send.at[n, g], down_recv.at[l - 1],
            at(jj=g * EIGHT + 2),
        )

    @pl.when(is3)
    def _():
        for b in range(len(plan.nodes)):
            take_rhs(b)
        pl.loop(0, len(plan.high))(take_block)
        for n, (l, a) in enumerate(plan.nodes):
            if n == 0 or plan.nodes[n - 1][0] != l:
                await_bytes(win.at[l - 4], w_recv.at[l - 4])
            total = rhs_t[n, c, z]
            for g in range(*plan.covers[a]):
                total = total - win[l - 4, g]
            for d in plan.below[a]:
                total = total - thin(fwd[plan.high_rhs[d]], block(plan.high[d, l]), NN)
            fwd[n] = thin(total, block(plan.high[a, 0]), NT)
        for l, a in reversed(plan.nodes):
            n = plan.high_rhs[a]
            rest = fwd[n]
            for k, up in plan.nodes:
                if a in plan.below[up]:
                    rest = rest - thin(xhigh[plan.high_rhs[up]], block(plan.high[a, k]), NT)
            xhigh[n] = thin(rest, block(plan.high[a, 0]), NN)
            for g in range(*plan.covers[a]):
                send_x(a, g).start()

    leaf_acc[...] = jnp.zeros_like(leaf_acc)

    def send_down(l, r, src=None):
        src = sol.at[l - 1] if src is None else src
        return remote(
            src, sol.at[l - 1], down_send.at[l - 1], down_recv.at[l - 1], at(jj=start + r)
        )

    def spread(l):
        full[l - 1, c, z] = sol[l - 1]
        for step in range(1, chips):
            remote(
                sol.at[l - 1], full.at[l - 1, c, z], ag_send.at[l - 1], ag_recv.at[l - 1],
                at(zz=turn(step)),
            ).start()

    def spread_left(step):
        return remote(
            sol.at[0], full.at[0, c, z], left_send, ag_recv.at[0], at(zz=turn(step), jj=mate)
        )

    @pl.when(is2)
    def _():
        rest = [fwd[0], fwd[1], fwd[2]]
        for l in range(top, 3, -1):
            await_bytes(sol.at[l - 1], down_recv.at[l - 1])
            for r in order:
                send_down(l, r).start()
            for n, key in enumerate((2, 6, 4)):
                rest[n] = rest[n] - thin(sol[l - 1], block(mid[key, l]), NT)
        sol[2] = thin(rest[2], block(mid[4, 0]), NN)
        for r in order:
            send_down(3, r).start()
        for n, key in enumerate((2, 6)):
            rest[n] = rest[n] - thin(sol[2], block(mid[key, 3]), NT)
        sol[1] = thin(rest[0], block(mid[2, 0]), NN)
        solb[...] = thin(rest[1], block(mid[6, 0]), NN)
        for r in order:
            send_down(2, r, None if r < 4 else solb).start()
        for l in range(top, 1, -1):
            spread(l)

    @pl.when(odd)
    def _():
        rest = fwd[0]
        for l in range(top, 1, -1):
            await_bytes(sol.at[l - 1], down_recv.at[l - 1])
            rest = rest - thin(sol[l - 1], block(l - 1), NT)
            if l > 3:
                spread(l)
        sol[0] = thin(rest, block(0), NN)
        spread(1)
        for step in range(chips):
            spread_left(step).start()
        for l in (3, 2):
            spread(l)

    @pl.when(jnp.logical_and(even, jnp.logical_not(is2)))
    def _():
        for l in range(top, 1, -1):
            await_bytes(sol.at[l - 1], down_recv.at[l - 1])
            spread(l)

    def pair(l):
        return remote(full.at[l, c], full.at[l, c], pair_send.at[l], pair_recv.at[l], at(cc=other))

    def leaf_back(l):
        await_bytes(full.at[l, other], pair_recv.at[l])
        ancestor = split(full[l].reshape(nrhs, width))
        leaf_acc[...] = leaf_acc[...] + mask_s[l].astype(F32) * product(
            ancestor, (p_hi[l], p_lo[l]), NT
        )

    @pl.loop(0, top)
    def _(i):
        l = top - 1 - i

        @pl.when(jnp.logical_and(l == 0, even))
        def _():
            await_bytes(full.at[0, c], ag_recv.at[0])

        @pl.when(jnp.logical_or(l > 0, odd))
        def _():
            await_bytes(full.at[l, c, 0 : chips - 1], ag_recv.at[l])

        pair(l).start()

        @pl.when(i >= 1)
        def _():
            leaf_back(l + 1)

    leaf_back(0)
    rest = split(leaf_t[...] - leaf_acc[...])
    leaf_out[...] = product(rest, (i_hi[...], i_lo[...])).T
    share_rows = inner_out.shape[0]
    turned[...] = full[lev - 1].reshape(nrhs, width).T
    inner_out[...] = turned[pl.ds(pl.multiple_of(member * share_rows, share_rows), share_rows), :]

    each_put(lambda copy: copy.wait_send())
    for buffer, _, send, _, give, _, _, every in kinds:
        @pl.loop(0, every)
        def _(b):
            await_bytes(buffer.at[b, 0 : chips - 1, 0], send.at[b])
            await_bytes(buffer.at[b, :, c], give.at[b])
    await_bytes(terms.at[0], t_send)
    await_bytes(pieces1.at[0, 0 : chips - 1], a1_send.at[0])
    await_bytes(pieces.at[0 : chips - 1], a_send)

    @pl.when(jnp.logical_not(is2))
    def _():
        for l in range(2, top + 1):
            send_v(l).wait_send()

    @pl.when(is2)
    def _():
        for l in range(4, top + 1):
            send_w(l).wait_send()
        for l in range(2, top + 1):
            await_bytes(vin.at[0, 0 : EIGHT - 1], down_send.at[l - 1])

    @pl.when(is3)
    def _():
        for l, a in plan.nodes:
            for g in range(*plan.covers[a]):
                send_x(a, g).wait_send()

    @pl.loop(1, top)
    def _(l):
        await_bytes(full.at[l, 0, 0 : chips - 1], ag_send.at[l])

    @pl.when(odd)
    def _():
        await_bytes(full.at[0, 0, 0 : chips - 1], ag_send.at[0])
        await_bytes(full.at[0, 0], left_send)

    @pl.when(even)
    def _():
        send_first(0).wait_send()

    @pl.loop(0, top)
    def _(l):
        pair(l).wait_send()


def per_device(leaf_rhs, leaf_inv, leaf_panel, leaf_mask, inner_rhs, inner_inv, inner_panel):
    members, count = lax.axis_size("grp"), lax.axis_size("row")
    chips = members // 2
    width, nrhs = leaf_rhs.shape[2:]
    top = leaf_panel.shape[2]
    share, cols = width // members, nrhs // members
    plan = Plan(top, count)
    nb, nr, high = plan.blocks, plan.rhs, top - 3
    hbm = pl.BlockSpec(memory_space=pl.ANY)
    dma = pltpu.SemaphoreType.DMA
    steps = max(chips // 2, 1)
    v = pltpu.VMEM
    call = pl.pallas_call(
        functools.partial(kernel, chips, count, plan),
        out_shape=(
            jax.ShapeDtypeStruct((width, nrhs), F32),
            jax.ShapeDtypeStruct((share, nrhs), F32),
        ),
        in_specs=[hbm, hbm, hbm, pl.BlockSpec(memory_space=pltpu.SMEM), hbm, hbm, hbm],
        out_specs=[pl.BlockSpec(memory_space=pltpu.VMEM)] * 2,
        scratch_shapes=[
            v((width, nrhs), F32),
            v((width, width), F32),
            v((top, width, width), F32),
            v((width, width), BF16),
            v((width, width), BF16),
            v((top, width, width), BF16),
            v((top, width, width), BF16),
            v((nrhs, width), F32),
            v((2, chips, top, cols, width), F32),
            v((chips, top, cols, width), F32),
            v((2, chips, cols, width), F32),
            v((chips, top - 1, cols, width), F32),
            v((top - 1, cols, width), F32),
            v((nb, chips, 2, share, width), F32),
            v((nr, chips, 2, share, nrhs), F32),
            v((nr, 2, chips, cols, width), F32),
            v((nb, width, width), BF16),
            v((nb, width, width), BF16),
            v((top - 1, EIGHT, cols, width), F32),
            v((high, plan.groups, cols, width), F32),
            v((high, cols, width), F32),
            v((nr, cols, width), F32),
            v((top, cols, width), F32),
            v((cols, width), F32),
            v((len(plan.nodes), cols, width), F32),
            v((top, 2, chips, cols, width), F32),
            v((nrhs, width), F32),
            v((width, nrhs), F32),
            dma((top + 2,)),
            dma((nb,)),
            dma((nr,)),
            dma((top + 1,)),
            dma((2, steps, nb)),
            dma((nb,)),
            dma((2, steps, nr)),
            dma((nr,)),
            dma((nb,)),
            dma((nb,)),
            dma((nr,)),
            dma((nr,)),
            dma((top,)),
            dma,
            dma((2,)),
            dma((2,)),
            dma,
            dma,
            dma((top - 1,)),
            dma((top - 1,)),
            dma((high,)),
            dma((high,)),
            dma((len(plan.nodes), plan.groups)),
            dma((top,)),
            dma((top,)),
            dma((top,)),
            dma((top,)),
            dma,
            dma((top,)),
            dma((top,)),
        ],
        compiler_params=pltpu.CompilerParams(
            collective_id=0, has_side_effects=True, vmem_limit_bytes=60 * 2**20
        ),
    )
    leaf, inner = call(
        leaf_rhs[0, 0], leaf_inv[0, 0], leaf_panel[0, 0], leaf_mask[0, 0],
        inner_rhs[0], inner_inv[0], inner_panel[0],
    )
    return leaf[None, None], inner[None]


def solution(mesh):
    in_specs = (
        P("row", "grp", None, None),
        P("row", "grp", None, None),
        P("row", "grp", None, None, None),
        P("row", "grp", None),
        P("row", "grp", None),
        P("row", "grp", None),
        P("row", None, "grp", None),
    )
    out_specs = (P("row", "grp", None, None), P("row", "grp", None))
    return jax.shard_map(
        per_device, mesh=mesh, in_specs=in_specs, out_specs=out_specs, check_vma=False
    )
```

time: 2120 us -> 83.5 us (0.04)
  blocking collectives: 1190 us -> 0 us
  waiting for transfers between devices: 881 us -> 0 us
  Pallas kernels: 0 us -> 79.5 us
  matrix products: 24.7 us -> 0 us
    psum x8 -> x0, blocking collectives: 689 us -> none  [the longest x4 353 us: per_device(): update = pick_slot(lax.psum(placed, 'row'), picks)]
    psum x4 -> x0, waiting for transfers between devices: 584 us -> none  [the longest x2 302 us: per_device(): update = pick_slot(lax.psum(placed, 'row'), picks)]
    all_gather x19 -> x0, blocking collectives: 501 us -> none  [the longest x6 200 us: per_device(): pending = lax.all_gather(inner_rhs[0] - update, 'grp', axis=0, tiled=True)]
    reduce_scatter x6 -> x0, waiting for transfers between devices: 297 us -> none  [per_device(): lax.psum_scatter(upward(jnp.int32(0), share * lax.axis_size('grp')), 'grp...]
    pallas_call x0 -> x1, Pallas kernels: none -> 79.5 us  [per_device(): call(leaf_rhs[0, 0], leaf_inv[0, 0], leaf_panel[0, 0], leaf_mask[0, 0], i...]
    dot_general x45 -> x0, matrix products: 24.7 us -> none  [the longest x6 7.51 us: upward(): jnp.einsum('lna,lnr->ar', masked_now, leaf_fwd, precision=highest)]
  transfers between devices with their start and end apart: 10 -> 0, of which waited for: 10 -> 0; matrix products, arithmetic and copies ran while one was open for 0% -> 0% of each run, Pallas kernels for 0% -> 0%
where the time goes in v2:
time: 83.5 us; the launch traced here: 83 us
  Pallas kernels  79.5 us (95%)
  local copies, waits for them, and re-layouts  2.86 us (3%)
    pallas_call x1, Pallas kernels, per_device(): call(leaf_rhs[0, 0], leaf_inv[0, 0], leaf_panel[0, 0], leaf_mask[0, 0], i...  79.5 us
    unnamed x2, local copies, waits for them, and re-layouts  2.86 us

profile of v2, /device:TPU:1, one launch (start us, length us, event | category | flops | bytes accessed | tf_op | source)
XLA Modules:
  0.0 83.0 jit_solution(14500048354116745276)
XLA Ops:
  0.6 79.5 %shard_map.86 = (f32[256,128]{1,0:T(8,128)}, f32[16,128]{1,0:T(8,128)}) custom-call(f32[256,128]{1,0:T(8,128)} %bitcast.11, f32[256,256]{1,0:T(8,128)} %bitcast.10, f32[6,256,256]{2,1,0:T(8,128)} %bitcast.9, s32[6]{0:T(128)} %bitcast.17, f32[16,128]{1,0:T(8,128)} %bitcast.15, f32[16,256]{1,0:T(8,128)} %bitcast.14, f32[6,16,256]{2,1,0:T(8,128)} %bitcast.13), custom_call_target="tpu_custom_call" | custom-call | tf_op jit(solution)/shard_map/pallas_call | solution.py:689
  80.1 1.6 %copy.11 = f32[1,1,256,128]{3,2,1,0:T(8,128)} copy(f32[1,1,256,128]{3,2,1,0:T(8,128)} %bitcast.12) | data formatting | bytes 262144
  81.7 1.3 %copy.12 = f32[1,16,128]{2,1,0:T(8,128)} copy(f32[1,16,128]{2,1,0:T(8,128)} %bitcast.16) | data formatting | bytes 16384

commit v3 on v2

--- a/solution.py
+++ b/solution.py
@@ -38,13 +38,14 @@
 class Plan:
     def __init__(self, top, count):
         self.groups = count // EIGHT
-        self.host3 = 14 if count > EIGHT else 6
-        order = [(2, 0)] + [(2, l) for l in range(3, top + 1)] + [(6, 0), (6, 3), (4, 0)]
-        for l in range(4, top + 1):
-            order += [(6, l), (4, l)]
+        self.host3 = 12 if count > EIGHT else 4
+        order = [(key, l) for key in (2, 6) for l in [0] + list(range(3, top + 1))]
+        order += [(4, l) for l in [0] + list(range(4, top + 1))]
         self.mid = {key: i for i, key in enumerate(order)}
-        self.mid_local = top - 1
         self.mid_rhs = {2: 0, 6: 1, 4: 2}
+        self.items = [(0, 2, 0, 4), (7, 2, 4, 4)]
+        for place, l in zip((6, 1, 5, 3), range(3, top + 1)):
+            self.items.append((place, l, 0, EIGHT))
         self.nodes = []
         for l in range(4, top):
             self.nodes += [(l, a) for a in range(2 ** (l - 1), count, 2**l)]
@@ -62,10 +63,10 @@
         order = []
         for l, a in self.nodes:
             order += [(d, l) for d in self.below[a]] + [(a, 0)]
-        self.high = {key: i for i, key in enumerate(order)}
-        self.high_rhs = {a: i for i, (l, a) in enumerate(self.nodes)}
-        self.blocks = max(top, len(self.mid), len(self.high))
-        self.rhs = max(3, len(self.nodes))
+        self.blocks = len(self.mid) + len(order)
+        self.high = {key: len(self.mid) + i for i, key in enumerate(order)}
+        self.rhs = 3 + len(self.nodes)
+        self.high_rhs = {a: 3 + i for i, (l, a) in enumerate(self.nodes)}
 
 
 def kernel(
@@ -73,12 +74,15 @@
     rhs_h, inv_h, pan_h, mask_s, irhs_h, iinv_h, ipan_h,
     leaf_out, inner_out,
     v_rhs, v_inv, v_pan, i_hi, i_lo, p_hi, p_lo, leaf_t,
-    terms, terms_in, pieces1, pieces, upd,
+    terms, terms_in, pieces1, upd,
+    gather, gsum, gchips, gout, tin,
     blocks, rblock, rhs_t, b_hi, b_lo,
     vin, win, wout, fwd, sol, solb, xhigh, full, leaf_acc, turned,
     in_sem, arr_sem, arr_rhs, put_send,
     ring_recv, ring_send, rring_recv, rring_send, sib_recv, sib_send, rsib_recv, rsib_send,
-    t_recv, t_send, a1_recv, a1_send, a_recv, a_send,
+    fw_recv, fw_send, rfw_recv, rfw_send,
+    t_recv, t_send, a1_recv, a1_send,
+    g_recv, g_send, gz_recv, gz_send, tin_recv, tin_send,
     v_recv, v_send, w_recv, w_send, x_send, down_recv, down_send,
     ag_recv, ag_send, left_send, pair_recv, pair_send,
 ):
@@ -100,10 +104,15 @@
     lev = jnp.int32(1)
     for bit in range(1, top):
         lev = lev + (lax.rem(j, 2**bit) == 0).astype(jnp.int32)
-    nblocks = jnp.where(odd, top, jnp.where(is2, len(plan.mid), jnp.where(is3, len(plan.high), 0)))
-    nlocal = jnp.where(odd, top, jnp.where(is2, plan.mid_local, 0))
-    nnodes = jnp.where(odd, 1, jnp.where(is2, 3, jnp.where(is3, len(plan.nodes), 0)))
-    nlocal_rhs = jnp.where(jnp.logical_or(odd, is2), 1, 0)
+    is0, is6 = place == 0, place == 6
+    helps = jnp.logical_or(is0, is6)
+    near = jnp.logical_not(jnp.logical_or(is0, place == 4))
+    low = jnp.where(is6, top - 1, jnp.where(is0, 2 * (top - 1), 0))
+    size = jnp.where(odd, top, jnp.where(is0, top - 2, top - 1))
+    size = jnp.where(place == 4, 0, size)
+    rlow = jnp.where(is6, 1, jnp.where(is0, 2, 0))
+    rsize = jnp.where(place == 4, 0, 1)
+    nmid = len(plan.mid)
 
     def at(zz=None, cc=None, jj=None):
         zz = z if zz is None else zz
@@ -144,14 +153,15 @@
         for l in [0] + list(range(2, top + 1)):
             keep(l, max(l - 1, 0))
 
-    @pl.when(is2)
-    def _():
-        for l in [0] + list(range(3, top + 1)):
-            keep(l, plan.mid[2, l])
-
-    @pl.when(jnp.logical_or(odd, is2))
-    def _():
-        local(irhs_h, rblock.at[0, z, c], arr_rhs.at[0]).start()
+    for key in (2, 6):
+        @pl.when(place == key)
+        def _(key=key):
+            for l in [0] + list(range(3, top + 1)):
+                keep(l, plan.mid[key, l])
+
+    @pl.when(near)
+    def _():
+        local(irhs_h, rblock.at[rlow, z, c], arr_rhs.at[rlow]).start()
 
     for step in range(1, top):
         panel_in(step).start()
@@ -167,16 +177,12 @@
     for step in range(chips):
         greet(at(zz=turn(step), jj=mate))
 
+    for step in range(1, EIGHT):
+        greet(at(jj=start + lax.rem(place + step, EIGHT)))
+
     @pl.when(is2)
     def _():
-        for r in range(EIGHT):
-            if r != 2:
-                greet(at(jj=start + r))
         greet(at(jj=plan.host3))
-
-    @pl.when(jnp.logical_not(is2))
-    def _():
-        greet(at(jj=host2))
 
     @pl.when(is3)
     def _():
@@ -185,14 +191,12 @@
         for l, a in plan.nodes:
             greet(at(jj=a))
 
-    @pl.when(place == 0)
+    @pl.when(is0)
     def _():
         greet(at(jj=plan.host3))
 
-    expected = 2 * chips + jnp.where(is2, EIGHT, 1)
+    expected = 2 * chips + EIGHT - 1 + jnp.where(is2, 1, 0) + jnp.where(is0, 1, 0)
     expected = expected + jnp.where(is3, plan.groups + len(plan.nodes), 0)
-    expected = expected + jnp.where(place == 0, 1, 0)
-    pl.semaphore_wait(barrier, expected)
 
     def puts(slots, rhs_slots, key, levels, target):
         for n, l in enumerate([0] + levels):
@@ -207,12 +211,10 @@
         )
 
     def each_put(act):
-        for key, l in ((6, 2), (4, 3)):
-            @pl.when(place == key)
-            def _(key=key, l=l):
-                levels = list(range(l + 1, top + 1))
-                for copy in puts(plan.mid, plan.mid_rhs, key, levels, host2):
-                    act(copy)
+        @pl.when(place == 4)
+        def _():
+            for copy in puts(plan.mid, plan.mid_rhs, 4, list(range(4, top + 1)), start):
+                act(copy)
         for l, a in plan.nodes:
             @pl.when(j == a)
             def _(l=l, a=a):
@@ -220,53 +222,80 @@
                 for copy in puts(plan.high, plan.high_rhs, a, levels, plan.host3):
                     act(copy)
 
-    each_put(lambda copy: copy.start())
-
     right, left = chips // 2, chips - 1 - chips // 2
 
-    def ring(buffer, send, recv, way, step, b):
-        src = turn(-step if way == 0 else step)
-        ref = buffer.at[b, src, c]
-        target = turn(1 if way == 0 else -1)
-        return remote(ref, ref, send.at[b], recv.at[way, step, b], at(zz=target))
-
-    def ring_arrived(buffer, recv, way, step, b):
-        src = turn(-step - 1 if way == 0 else step + 1)
-        await_bytes(buffer.at[b, src, c], recv.at[way, step, b])
+    def heading(way, b):
+        return (1 if way == 0 else -1) * (1 - 2 * lax.rem(b, 2))
+
+    def ring(kind, way, step, b):
+        ref = kind[0].at[b, turn(-step * heading(way, b)), c]
+        return remote(
+            ref, ref, kind[2].at[b], kind[3].at[way, step, b], at(zz=turn(heading(way, b)))
+        )
+
+    def ring_arrived(kind, way, step, b):
+        src = turn(-(step + 1) * heading(way, b))
+        await_bytes(kind[0].at[b, src, c], kind[3].at[way, step, b])
+        pass_on(kind, b, src)
 
     kinds = (
-        (blocks, arr_sem, ring_send, ring_recv, sib_send, sib_recv, nlocal, nblocks),
-        (rblock, arr_rhs, rring_send, rring_recv, rsib_send, rsib_recv, nlocal_rhs, nnodes),
+        (blocks, arr_sem, ring_send, ring_recv, sib_send, sib_recv, fw_send, fw_recv),
+        (rblock, arr_rhs, rring_send, rring_recv, rsib_send, rsib_recv, rfw_send, rfw_recv),
     )
-
-    def first_step(near):
-        for buffer, arrived, send, recv, _, _, mine, every in kinds:
-            @pl.loop(0 if near else mine, mine if near else every)
+    ranges = ((low, low + size), (rlow, rlow + rsize))
+    ranges3 = (
+        (nmid, jnp.where(is3, plan.blocks, nmid)),
+        (3, jnp.where(is3, plan.rhs, 3)),
+    )
+
+    def pass_on(kind, b, src):
+        @pl.when(passes(kind, b))
+        def _():
+            ref = kind[0].at[b, src, c]
+            remote(ref, ref, kind[6].at[b], kind[7].at[b], at(jj=host2)).start()
+
+    def first_step(ranges):
+        for kind, (first, last) in zip(kinds, ranges):
+            @pl.loop(first, last)
             def _(b):
-                await_bytes(buffer.at[b, z, c], arrived.at[b])
+                await_bytes(kind[0].at[b, z, c], kind[1].at[b])
                 if right:
-                    ring(buffer, send, recv, 0, 0, b).start()
+                    ring(kind, 0, 0, b).start()
                 if left:
-                    ring(buffer, send, recv, 1, 0, b).start()
-
-    def next_step(step):
-        for buffer, _, send, recv, give, got, _, every in kinds:
-            @pl.loop(0, every)
+                    ring(kind, 1, 0, b).start()
+                pass_on(kind, b, z)
+
+    final = max(right, left)
+
+    def next_step(step, ranges):
+        for kind, (first, last) in zip(kinds, ranges):
+            @pl.loop(first, last)
             def _(b):
                 if step <= right:
-                    ring_arrived(buffer, recv, 0, step - 1, b)
+                    ring_arrived(kind, 0, step - 1, b)
                     if step < right:
-                        ring(buffer, send, recv, 0, step, b).start()
+                        ring(kind, 0, step, b).start()
                 if step <= left:
-                    ring_arrived(buffer, recv, 1, step - 1, b)
+                    ring_arrived(kind, 1, step - 1, b)
                     if step < left:
-                        ring(buffer, send, recv, 1, step, b).start()
-                if step == max(right, left):
-                    share(buffer, give, got, b).start()
-
-    def share(buffer, send, recv, b):
-        ref = buffer.at[b, :, c]
-        return remote(ref, ref, send.at[b], recv.at[b], at(cc=other))
+                        ring(kind, 1, step, b).start()
+                if step == final:
+                    @pl.when(jnp.logical_not(passes(kind, b)))
+                    def _():
+                        share(kind, b).start()
+
+    def passes(kind, b):
+        return jnp.logical_and(helps, b < (nmid if kind[0] is blocks else 3))
+
+    def share(kind, b):
+        ref = kind[0].at[b, :, c]
+        return remote(ref, ref, kind[4].at[b], kind[5].at[b], at(cc=other))
+
+    def helped(kind, first, last):
+        @pl.loop(first, last)
+        def _(b):
+            await_bytes(kind[0].at[b, :, c], kind[7].at[b])
+            share(kind, b).start()
 
     def take_rhs(b):
         await_bytes(rblock.at[b, :, other], rsib_recv.at[b])
@@ -280,8 +309,6 @@
 
     def block(b):
         return b_hi[b], b_lo[b]
-
-    first_step(True)
 
     rhs_in.wait()
     inv_in.wait()
@@ -305,7 +332,14 @@
         p_lo[l] = lo
         term = product(forward, (hi, lo)) * mask_s[l].astype(F32)
         terms[:, :, l] = term.reshape(2, chips, -1, width)
+
+    pl.semaphore_wait(barrier, expected)
+
+    for l in range(top):
         swap_cores(l).start()
+    each_put(lambda copy: copy.start())
+    nowhere = lambda pair: (pair[0], jnp.where(near, pair[1], pair[0]))
+    first_step([nowhere(pair) for pair in ranges])
 
     def add_cores(l):
         await_bytes(terms_in.at[:, l], t_recv.at[l])
@@ -326,46 +360,87 @@
     for step in range(1, chips):
         send_first(step).start()
 
-    pl.loop(1, top)(add_cores)
-    for step in range(1, chips):
-        remote(
-            terms.at[c, turn(step), 1:top], pieces.at[z], a_send, a_recv, at(zz=turn(step))
-        ).start()
-
-    first_step(False)
-    for step in range(1, max(right, left)):
-        next_step(step)
-
-    @pl.when(odd)
-    def _():
-        next_step(max(right, left))
-
-    def own_sum():
-        await_bytes(pieces.at[0 : chips - 1], a_recv)
-        total = terms[c, z, 1:top]
-        for step in range(1, chips):
-            total = total + pieces[turn(step)]
-        upd[...] = total
+    def collect(i):
+        at_place, l, first, n = plan.items[i]
+        return remote(
+            terms.at[c, :, l - 1], gather.at[place], g_send.at[i], g_recv, at(jj=start + at_place)
+        )
+
+    def each_collect(l, act):
+        for i, (at_place, level, first, n) in enumerate(plan.items):
+            if level == l:
+                @pl.when(jnp.logical_and(
+                    place != at_place, jnp.logical_and(place >= first, place < first + n)
+                ))
+                def _(i=i):
+                    act(collect(i))
+
+    for l in range(2, top + 1):
+        add_cores(l - 1)
+        each_collect(l, lambda copy: copy.start())
+
+    holds, my_item, my_level = place < 0, jnp.int32(0), jnp.int32(0)
+    for i, (at_place, l, first, n) in enumerate(plan.items):
+        mine = place == at_place
+        holds = jnp.logical_or(holds, mine)
+        my_item = jnp.where(mine, i, my_item)
+        my_level = jnp.where(mine, l - 1, my_level)
+    sources = jnp.where(my_item < 2, 4, EIGHT)
+    origin = jnp.where(my_item == 1, 4, 0)
+
+    def to_chip(step):
+        return remote(gsum.at[turn(step)], gchips.at[z], gz_send, gz_recv, at(zz=turn(step)))
+
+    def to_host():
+        return remote(gout, tin.at[my_item], tin_send, tin_recv.at[my_item], at(jj=host2))
+
+    def sum_places():
+        @pl.when(holds)
+        def _():
+            @pl.when(my_item < 2)
+            def _():
+                await_bytes(gather.at[0:3], g_recv)
+
+            @pl.when(my_item >= 2)
+            def _():
+                await_bytes(gather.at[0 : EIGHT - 1], g_recv)
+
+            gsum[...] = terms[c, :, my_level]
+
+            @pl.loop(1, sources)
+            def _(k):
+                r = origin + lax.rem(place - origin + k, sources)
+                gsum[...] = gsum[...] + gather[r]
+
+            for step in range(1, chips):
+                to_chip(step).start()
+
+    def sum_chips():
+        @pl.when(holds)
+        def _():
+            await_bytes(gchips.at[0 : chips - 1], gz_recv)
+            total = gsum[z]
+            for step in range(1, chips):
+                total = total + gchips[turn(step)]
+            gout[...] = total
+            to_host().start()
+
+    far = lambda pair: (pair[0], jnp.where(near, pair[0], pair[1]))
+    first_step([far(pair) for pair in ranges])
+    first_step(ranges3)
+    between = (final + 1) // 2
+    for step in range(1, final + 1):
+        next_step(step, ranges)
+        next_step(step, ranges3)
+        if step == between:
+            sum_places()
+    sum_chips()
 
     def send_v(l):
         return remote(
-            upd.at[l - 2], vin.at[l - 2, place], v_send.at[l - 2], v_recv.at[l - 2], at(jj=host2)
-        )
-
-    @pl.when(even)
-    def _():
-        own_sum()
-
-        @pl.when(is2)
-        def _():
-            vin[:, 2] = upd[...]
-
-        @pl.when(jnp.logical_not(is2))
-        def _():
-            for l in range(2, top + 1):
-                send_v(l).start()
-
-        next_step(max(right, left))
+            upd.at[l - 2], vin.at[l - 2, lax.div(place, 2)], v_send.at[l - 2], v_recv.at[l - 2],
+            at(jj=host2),
+        )
 
     @pl.when(odd)
     def _():
@@ -377,12 +452,10 @@
         for step in range(1, chips):
             total = total + (pieces1[0, turn(step)] + pieces1[1, turn(step)])
         fwd[0] = thin(rhs_t[0, c, z] - total, block(0), NT)
-        own_sum()
-
         @pl.loop(2, top + 1)
         def _(l):
             take_block(l - 1)
-            upd[l - 2] = upd[l - 2] + thin(fwd[0], block(l - 1), NN)
+            upd[l - 2] = thin(fwd[0], block(l - 1), NN)
             send_v(l).start()
 
     mid = plan.mid
@@ -395,31 +468,36 @@
         )
 
     def arrived(l):
-        await_bytes(vin.at[l - 2, 0 : EIGHT - 1], v_recv.at[l - 2])
+        await_bytes(vin.at[l - 2], v_recv.at[l - 2])
+        for i, item in enumerate(plan.items):
+            if item[1] == l:
+                await_bytes(tin.at[i], tin_recv.at[i])
 
     def slots(l, first, last):
-        total = vin[l - 2, first]
-        for r in range(first + 1, last):
+        total = tin[l - 1 if l > 2 else first // 2]
+        for r in range(first, last):
             total = total + vin[l - 2, r]
         return total
 
     @pl.when(is2)
     def _():
+        helped(kinds[1], 1, 3)
+        helped(kinds[0], top - 1, nmid)
         for b in range(3):
             take_rhs(b)
-        pl.loop(0, len(mid))(take_block)
+        pl.loop(0, nmid)(take_block)
         arrived(2)
-        fwd[0] = thin(rhs_t[0, c, z] - slots(2, 0, 4), block(mid[2, 0]), NT)
-        fwd[1] = thin(rhs_t[1, c, z] - slots(2, 4, 8), block(mid[6, 0]), NT)
+        fwd[0] = thin(rhs_t[0, c, z] - slots(2, 0, 2), block(mid[2, 0]), NT)
+        fwd[1] = thin(rhs_t[1, c, z] - slots(2, 2, 4), block(mid[6, 0]), NT)
         arrived(3)
         fwd[2] = thin(
-            rhs_t[2, c, z] - slots(3, 0, 8) - thin(fwd[0], block(mid[2, 3]), NN)
+            rhs_t[2, c, z] - slots(3, 0, 4) - thin(fwd[0], block(mid[2, 3]), NN)
             - thin(fwd[1], block(mid[6, 3]), NN),
             block(mid[4, 0]), NT,
         )
         for l in range(4, top + 1):
             arrived(l)
-            wout[l - 4] = slots(l, 0, 8) + (
+            wout[l - 4] = slots(l, 0, 4) + (
                 thin(fwd[0], block(mid[2, l]), NN) + thin(fwd[1], block(mid[6, l]), NN)
             ) + thin(fwd[2], block(mid[4, l]), NN)
             send_w(l).start()
@@ -427,7 +505,7 @@
     level_of = {a: l for l, a in plan.nodes}
 
     def send_x(a, g):
-        n = plan.high_rhs[a]
+        n = plan.high_rhs[a] - 3
         l = level_of[a]
         return remote(
             xhigh.at[n], sol.at[l - 1], x_send.at[n, g], down_recv.at[l - 1],
@@ -436,24 +514,24 @@
 
     @pl.when(is3)
     def _():
-        for b in range(len(plan.nodes)):
+        for b in range(3, plan.rhs):
             take_rhs(b)
-        pl.loop(0, len(plan.high))(take_block)
+        pl.loop(nmid, plan.blocks)(take_block)
         for n, (l, a) in enumerate(plan.nodes):
             if n == 0 or plan.nodes[n - 1][0] != l:
                 await_bytes(win.at[l - 4], w_recv.at[l - 4])
-            total = rhs_t[n, c, z]
+            total = rhs_t[3 + n, c, z]
             for g in range(*plan.covers[a]):
                 total = total - win[l - 4, g]
             for d in plan.below[a]:
-                total = total - thin(fwd[plan.high_rhs[d]], block(plan.high[d, l]), NN)
+                total = total - thin(fwd[plan.high_rhs[d] - 3], block(plan.high[d, l]), NN)
             fwd[n] = thin(total, block(plan.high[a, 0]), NT)
         for l, a in reversed(plan.nodes):
-            n = plan.high_rhs[a]
+            n = plan.high_rhs[a] - 3
             rest = fwd[n]
             for k, up in plan.nodes:
                 if a in plan.below[up]:
-                    rest = rest - thin(xhigh[plan.high_rhs[up]], block(plan.high[a, k]), NT)
+                    rest = rest - thin(xhigh[plan.high_rhs[up] - 3], block(plan.high[a, k]), NT)
             xhigh[n] = thin(rest, block(plan.high[a, 0]), NN)
             for g in range(*plan.covers[a]):
                 send_x(a, g).start()
@@ -557,16 +635,38 @@
     inner_out[...] = turned[pl.ds(pl.multiple_of(member * share_rows, share_rows), share_rows), :]
 
     each_put(lambda copy: copy.wait_send())
-    for buffer, _, send, _, give, _, _, every in kinds:
-        @pl.loop(0, every)
-        def _(b):
-            await_bytes(buffer.at[b, 0 : chips - 1, 0], send.at[b])
-            await_bytes(buffer.at[b, :, c], give.at[b])
+    for some in (ranges, ranges3):
+        for kind, (first, last) in zip(kinds, some):
+            @pl.loop(first, last)
+            def _(b):
+                await_bytes(kind[0].at[b, 0 : chips - 1, 0], kind[2].at[b])
+                gone = jnp.where(passes(kind, b), 1, 0)
+
+                @pl.when(gone == 1)
+                def _():
+                    await_bytes(kind[0].at[b, :, c], kind[6].at[b])
+
+                @pl.when(gone == 0)
+                def _():
+                    await_bytes(kind[0].at[b, :, c], kind[4].at[b])
+
+    @pl.when(is2)
+    def _():
+        for kind, (first, last) in zip(kinds, ((top - 1, nmid), (1, 3))):
+            @pl.loop(first, last)
+            def _(b):
+                await_bytes(kind[0].at[b, :, c], kind[4].at[b])
     await_bytes(terms.at[0], t_send)
     await_bytes(pieces1.at[0, 0 : chips - 1], a1_send.at[0])
-    await_bytes(pieces.at[0 : chips - 1], a_send)
-
-    @pl.when(jnp.logical_not(is2))
+    for l in range(2, top + 1):
+        each_collect(l, lambda copy: copy.wait_send())
+
+    @pl.when(holds)
+    def _():
+        await_bytes(gchips.at[0 : chips - 1], gz_send)
+        to_host().wait_send()
+
+    @pl.when(odd)
     def _():
         for l in range(2, top + 1):
             send_v(l).wait_send()
@@ -576,7 +676,7 @@
         for l in range(4, top + 1):
             send_w(l).wait_send()
         for l in range(2, top + 1):
-            await_bytes(vin.at[0, 0 : EIGHT - 1], down_send.at[l - 1])
+            await_bytes(gather.at[0 : EIGHT - 1, 0], down_send.at[l - 1])
 
     @pl.when(is3)
     def _():
@@ -634,17 +734,21 @@
             v((2, chips, top, cols, width), F32),
             v((chips, top, cols, width), F32),
             v((2, chips, cols, width), F32),
-            v((chips, top - 1, cols, width), F32),
             v((top - 1, cols, width), F32),
+            v((EIGHT, chips, cols, width), F32),
+            v((chips, cols, width), F32),
+            v((chips, cols, width), F32),
+            v((cols, width), F32),
+            v((top, cols, width), F32),
             v((nb, chips, 2, share, width), F32),
             v((nr, chips, 2, share, nrhs), F32),
             v((nr, 2, chips, cols, width), F32),
             v((nb, width, width), BF16),
             v((nb, width, width), BF16),
-            v((top - 1, EIGHT, cols, width), F32),
+            v((top - 1, 4, cols, width), F32),
             v((high, plan.groups, cols, width), F32),
             v((high, cols, width), F32),
-            v((nr, cols, width), F32),
+            v((max(3, len(plan.nodes)), cols, width), F32),
             v((top, cols, width), F32),
             v((cols, width), F32),
             v((len(plan.nodes), cols, width), F32),
@@ -663,11 +767,19 @@
             dma((nb,)),
             dma((nr,)),
             dma((nr,)),
+            dma((nb,)),
+            dma((nb,)),
+            dma((3,)),
+            dma((3,)),
             dma((top,)),
             dma,
             dma((2,)),
             dma((2,)),
             dma,
+            dma((top,)),
+            dma,
+            dma,
+            dma((top,)),
             dma,
             dma((top - 1,)),
             dma((top - 1,)),

time: 83.5 us -> 75.3 us (0.902)
  Pallas kernels: 79.5 us -> 71.3 us
    pallas_call x1, Pallas kernels: 79.5 us -> 71.3 us  [per_device(): call(leaf_rhs[0, 0], leaf_inv[0, 0], leaf_panel[0, 0], leaf_mask[0, 0], i...]
where the time goes in v3:
time: 75.3 us; the launch traced here: 74.8 us
  Pallas kernels  71.3 us (95%)
  local copies, waits for them, and re-layouts  2.86 us (4%)
    pallas_call x1, Pallas kernels, per_device(): call(leaf_rhs[0, 0], leaf_inv[0, 0], leaf_panel[0, 0], leaf_mask[0, 0], i...  71.3 us
    unnamed x2, local copies, waits for them, and re-layouts  2.86 us

profile of v3, /device:TPU:1, one launch (start us, length us, event | category | flops | bytes accessed | tf_op | source)
XLA Modules:
  0.0 74.8 jit_solution(16954894493529381965)
XLA Ops:
  0.6 71.3 %shard_map.86 = (f32[256,128]{1,0:T(8,128)}, f32[16,128]{1,0:T(8,128)}) custom-call(f32[256,128]{1,0:T(8,128)} %bitcast.11, f32[256,256]{1,0:T(8,128)} %bitcast.10, f32[6,256,256]{2,1,0:T(8,128)} %bitcast.9, s32[6]{0:T(128)} %bitcast.17, f32[16,128]{1,0:T(8,128)} %bitcast.15, f32[16,256]{1,0:T(8,128)} %bitcast.14, f32[6,16,256]{2,1,0:T(8,128)} %bitcast.13), custom_call_target="tpu_custom_call" | custom-call | tf_op jit(solution)/shard_map/pallas_call | solution.py:801
  72.0 1.6 %copy.11 = f32[1,1,256,128]{3,2,1,0:T(8,128)} copy(f32[1,1,256,128]{3,2,1,0:T(8,128)} %bitcast.12) | data formatting | bytes 262144
  73.5 1.3 %copy.12 = f32[1,16,128]{2,1,0:T(8,128)} copy(f32[1,16,128]{2,1,0:T(8,128)} %bitcast.16) | data formatting | bytes 16384

commit v4 on v3

--- a/solution.py
+++ b/solution.py
@@ -717,8 +717,8 @@
     call = pl.pallas_call(
         functools.partial(kernel, chips, count, plan),
         out_shape=(
-            jax.ShapeDtypeStruct((width, nrhs), F32),
-            jax.ShapeDtypeStruct((share, nrhs), F32),
+            pltpu.VMEM((width, nrhs), F32),
+            pltpu.VMEM((share, nrhs), F32),
         ),
         in_specs=[hbm, hbm, hbm, pl.BlockSpec(memory_space=pltpu.SMEM), hbm, hbm, hbm],
         out_specs=[pl.BlockSpec(memory_space=pltpu.VMEM)] * 2,

time: 75.3 us -> 73 us (0.969)
  local copies, waits for them, and re-layouts: 2.86 us -> 1.26 us
    unnamed x2, local copies, waits for them, and re-layouts: 2.86 us -> 1.26 us
where the time goes in v4:
time: 73 us; the launch traced here: 72.6 us
  Pallas kernels  70.7 us (97%)
  local copies, waits for them, and re-layouts  1.26 us (2%)
    pallas_call x1, Pallas kernels, per_device(): call(leaf_rhs[0, 0], leaf_inv[0, 0], leaf_panel[0, 0], leaf_mask[0, 0], i...  70.7 us

profile of v4, /device:TPU:1, one launch (start us, length us, event | category | flops | bytes accessed | tf_op | source)
XLA Modules:
  0.0 72.6 jit_solution(5846137731249114593)
XLA Ops:
  0.6 70.7 %shard_map.86 = (f32[256,128]{1,0:T(8,128)S(1)}, f32[16,128]{1,0:T(8,128)S(1)}) custom-call(f32[256,128]{1,0:T(8,128)} %bitcast.13, f32[256,256]{1,0:T(8,128)} %bitcast.12, f32[6,256,256]{2,1,0:T(8,128)} %bitcast.11, s32[6]{0:T(128)} %bitcast.17, f32[16,128]{1,0:T(8,128)} %bitcast.16, f32[16,256]{1,0:T(8,128)} %bitcast.15, f32[6,16,256]{2,1,0:T(8,128)} %bitcast.14), custom_call_target="tpu_custom_call" | custom-call | tf_op jit(solution)/shard_map/pallas_call | solution.py:801
  71.3 0.7 copy.11
  72.0 0.6 copy.12

commit v5 on v4

--- a/solution.py
+++ b/solution.py
@@ -43,6 +43,7 @@
         order += [(4, l) for l in [0] + list(range(4, top + 1))]
         self.mid = {key: i for i, key in enumerate(order)}
         self.mid_rhs = {2: 0, 6: 1, 4: 2}
+        self.lent = 2
         self.items = [(0, 2, 0, 4), (7, 2, 4, 4)]
         for place, l in zip((6, 1, 5, 3), range(3, top + 1)):
             self.items.append((place, l, 0, EIGHT))
@@ -107,9 +108,11 @@
     is0, is6 = place == 0, place == 6
     helps = jnp.logical_or(is0, is6)
     near = jnp.logical_not(jnp.logical_or(is0, place == 4))
-    low = jnp.where(is6, top - 1, jnp.where(is0, 2 * (top - 1), 0))
-    size = jnp.where(odd, top, jnp.where(is0, top - 2, top - 1))
-    size = jnp.where(place == 4, 0, size)
+    lent = top - 1 + plan.lent
+    low = jnp.where(is6, lent, jnp.where(is0, 2 * (top - 1), 0))
+    size = jnp.where(odd, top, jnp.where(is0, top - 2, 2 * (top - 1) - lent))
+    size = jnp.where(is2, lent, jnp.where(place == 4, 0, size))
+    here = jnp.where(is0, 0, jnp.where(is2, top - 1, size))
     rlow = jnp.where(is6, 1, jnp.where(is0, 2, 0))
     rsize = jnp.where(place == 4, 0, 1)
     nmid = len(plan.mid)
@@ -156,7 +159,7 @@
     for key in (2, 6):
         @pl.when(place == key)
         def _(key=key):
-            for l in [0] + list(range(3, top + 1)):
+            for l in ([0] + list(range(3, top + 1)))[0 if key == 2 else plan.lent :]:
                 keep(l, plan.mid[key, l])
 
     @pl.when(near)
@@ -211,6 +214,15 @@
         )
 
     def each_put(act):
+        @pl.when(place == 6)
+        def _():
+            for n, l in enumerate(([0] + list(range(3, top + 1)))[: plan.lent]):
+                src = iinv_h if l == 0 else ipan_h.at[l - 1]
+                slot = plan.mid[6, l]
+                act(remote(
+                    src, blocks.at[slot, z, c], put_send.at[n], arr_sem.at[slot], at(jj=host2)
+                ))
+
         @pl.when(place == 4)
         def _():
             for copy in puts(plan.mid, plan.mid_rhs, 4, list(range(4, top + 1)), start):
@@ -338,8 +350,8 @@
     for l in range(top):
         swap_cores(l).start()
     each_put(lambda copy: copy.start())
-    nowhere = lambda pair: (pair[0], jnp.where(near, pair[1], pair[0]))
-    first_step([nowhere(pair) for pair in ranges])
+    rhere = jnp.where(near, rsize, 0)
+    first_step([(low, low + here), (rlow, rlow + rhere)])
 
     def add_cores(l):
         await_bytes(terms_in.at[:, l], t_recv.at[l])
@@ -425,8 +437,7 @@
             gout[...] = total
             to_host().start()
 
-    far = lambda pair: (pair[0], jnp.where(near, pair[0], pair[1]))
-    first_step([far(pair) for pair in ranges])
+    first_step([(low + here, low + size), (rlow + rhere, rlow + rsize)])
     first_step(ranges3)
     between = (final + 1) // 2
     for step in range(1, final + 1):
@@ -482,7 +493,7 @@
     @pl.when(is2)
     def _():
         helped(kinds[1], 1, 3)
-        helped(kinds[0], top - 1, nmid)
+        helped(kinds[0], lent, nmid)
         for b in range(3):
             take_rhs(b)
         pl.loop(0, nmid)(take_block)
@@ -566,6 +577,8 @@
                 send_down(l, r).start()
             for n, key in enumerate((2, 6, 4)):
                 rest[n] = rest[n] - thin(sol[l - 1], block(mid[key, l]), NT)
+            if l > 4:
+                spread(l)
         sol[2] = thin(rest[2], block(mid[4, 0]), NN)
         for r in order:
             send_down(3, r).start()
@@ -575,7 +588,7 @@
         solb[...] = thin(rest[1], block(mid[6, 0]), NN)
         for r in order:
             send_down(2, r, None if r < 4 else solb).start()
-        for l in range(top, 1, -1):
+        for l in range(min(top, 4), 1, -1):
             spread(l)
 
     @pl.when(odd)
@@ -652,7 +665,7 @@
 
     @pl.when(is2)
     def _():
-        for kind, (first, last) in zip(kinds, ((top - 1, nmid), (1, 3))):
+        for kind, (first, last) in zip(kinds, ((lent, nmid), (1, 3))):
             @pl.loop(first, last)
             def _(b):
                 await_bytes(kind[0].at[b, :, c], kind[4].at[b])

time: 73 us -> 72.9 us (level)
  no operation moved by 1% of the time
where the time goes in v5:
time: 72.9 us; the launch traced here: 72.8 us
  Pallas kernels  70.9 us (97%)
  local copies, waits for them, and re-layouts  1.26 us (2%)
    pallas_call x1, Pallas kernels, per_device(): call(leaf_rhs[0, 0], leaf_inv[0, 0], leaf_panel[0, 0], leaf_mask[0, 0], i...  70.9 us

profile of v5, /device:TPU:1, one launch (start us, length us, event | category | flops | bytes accessed | tf_op | source)
XLA Modules:
  0.0 72.8 jit_solution(6415541694958728273)
XLA Ops:
  0.6 70.9 %shard_map.86 = (f32[256,128]{1,0:T(8,128)S(1)}, f32[16,128]{1,0:T(8,128)S(1)}) custom-call(f32[256,128]{1,0:T(8,128)} %bitcast.13, f32[256,256]{1,0:T(8,128)} %bitcast.12, f32[6,256,256]{2,1,0:T(8,128)} %bitcast.11, s32[6]{0:T(128)} %bitcast.17, f32[16,128]{1,0:T(8,128)} %bitcast.16, f32[16,256]{1,0:T(8,128)} %bitcast.15, f32[6,16,256]{2,1,0:T(8,128)} %bitcast.14), custom_call_target="tpu_custom_call" | custom-call | tf_op jit(solution)/shard_map/pallas_call | solution.py:814
  71.5 0.7 copy.11
  72.2 0.6 copy.12

commit v6 on v4

--- a/solution.py
+++ b/solution.py
@@ -566,6 +566,8 @@
                 send_down(l, r).start()
             for n, key in enumerate((2, 6, 4)):
                 rest[n] = rest[n] - thin(sol[l - 1], block(mid[key, l]), NT)
+            if l > 4:
+                spread(l)
         sol[2] = thin(rest[2], block(mid[4, 0]), NN)
         for r in order:
             send_down(3, r).start()
@@ -575,7 +577,7 @@
         solb[...] = thin(rest[1], block(mid[6, 0]), NN)
         for r in order:
             send_down(2, r, None if r < 4 else solb).start()
-        for l in range(top, 1, -1):
+        for l in range(min(top, 4), 1, -1):
             spread(l)
 
     @pl.when(odd)
@@ -627,12 +629,17 @@
         def _():
             leaf_back(l + 1)
 
+    def own_rows():
+        share_rows = inner_out.shape[0]
+        turned[...] = full[lev - 1].reshape(nrhs, width).T
+        rows = pl.ds(pl.multiple_of(member * share_rows, share_rows), share_rows)
+        inner_out[...] = turned[rows, :]
+
+    pl.when(even)(own_rows)
     leaf_back(0)
     rest = split(leaf_t[...] - leaf_acc[...])
     leaf_out[...] = product(rest, (i_hi[...], i_lo[...])).T
-    share_rows = inner_out.shape[0]
-    turned[...] = full[lev - 1].reshape(nrhs, width).T
-    inner_out[...] = turned[pl.ds(pl.multiple_of(member * share_rows, share_rows), share_rows), :]
+    pl.when(odd)(own_rows)
 
     each_put(lambda copy: copy.wait_send())
     for some in (ranges, ranges3):

time: 73 us -> 73 us (level)
  no operation moved by 1% of the time
where the time goes in v6:
time: 73 us; the launch traced here: 72.5 us
  Pallas kernels  70.7 us (97%)
  local copies, waits for them, and re-layouts  1.26 us (2%)
    pallas_call x1, Pallas kernels, per_device(): call(leaf_rhs[0, 0], leaf_inv[0, 0], leaf_panel[0, 0], leaf_mask[0, 0], i...  70.7 us

profile of v6, /device:TPU:1, one launch (start us, length us, event | category | flops | bytes accessed | tf_op | source)
XLA Modules:
  0.0 72.5 jit_solution(3033767384482580293)
XLA Ops:
  0.6 70.7 %shard_map.86 = (f32[256,128]{1,0:T(8,128)S(1)}, f32[16,128]{1,0:T(8,128)S(1)}) custom-call(f32[256,128]{1,0:T(8,128)} %bitcast.13, f32[256,256]{1,0:T(8,128)} %bitcast.12, f32[6,256,256]{2,1,0:T(8,128)} %bitcast.11, s32[6]{0:T(128)} %bitcast.17, f32[16,128]{1,0:T(8,128)} %bitcast.16, f32[16,256]{1,0:T(8,128)} %bitcast.15, f32[6,16,256]{2,1,0:T(8,128)} %bitcast.14), custom_call_target="tpu_custom_call" | custom-call | tf_op jit(solution)/shard_map/pallas_call | solution.py:808
  71.3 0.7 copy.11
  71.9 0.6 copy.12
